TPU v7x, 512 devices: a whole 4x4x16 slice. The times are simulated.
512 devices in a mesh: region: 128 (over x, z, core), chan: 4 (over y).
Axes of the slice: x: 4, y: 4, z: 16, core: 2. Of those that a mesh axis runs over, the one named last changes fastest.
Arguments:
- sky_maps: bfloat16 [128, 65536], P('chan', 'region'), may hold values from -6 to 6
- neighbours: int32 [8, 65536], P(None, 'region'), may hold values from 0 to 768, as said below
- send_lists: int32 [2, 16384], P(None, 'region'), may hold values from 0 to 511, as said below
- counts: int32 [128], replicated, may hold values from 171 to 511, as said below
- cheb_weight: bfloat16 [4, 128, 128], P(None, 'chan'), may hold values from -0.25 to 0.25
- first_weight: bfloat16 [128, 512], P(None, 'chan'), may hold values from -0.5 to 0.5
- second_weight: bfloat16 [512, 64], P('chan'), may hold values from -0.25 to 0.25
- cotangent: bfloat16 [64, 32768], P('chan', 'region'), may hold values from -6 to 6
Outputs:
- mlp_out: bfloat16 [64, 32768], P('chan', 'region')
- input_grad: float32 [128, 65536], P('chan', 'region')
- cheb_grad: float32 [4, 128, 128], P(None, 'chan')
- first_grad: float32 [128, 512], P(None, 'chan')
- second_grad: float32 [512, 64], P('chan')
Inputs may be any that keep to these rules, and one draw needn't show every extreme that they name: Patch i observes its pixel slots 0 to counts[i] - 1 and no others; the counts sum to 32768. Column p of patch i lists up to eight neighbours of slot p in the encoding of the operator P; links join observed slots only and are symmetric, across patches too. `send_lists`: each row of a patch's send lists holds 128 distinct slots of that patch.
All inputs are finite; a program needn't handle non-finite values.
Results may differ from a plain program's by a relative error of at most 0.025.
Values may be sent and summed in bfloat16 or wider, within the bound.
A program may use at most 64 MiB of HBM per device.

v0:
```python
import math

import jax
import jax.numpy as jnp
from jax import lax
from jax.sharding import PartitionSpec as P

MOST = 511


def extended_2(cells, sides, width):
    for axis, dim in sides:
        count = lax.axis_size(axis)
        ends = count - 1
        head = lax.slice_in_dim(cells, 0, width, axis=dim)
        tail = lax.slice_in_dim(cells, cells.shape[dim] - width, cells.shape[dim], axis=dim)
        cells = jnp.concatenate(
            [
                lax.ppermute(tail, axis, [(i, (i + 1) % count) for i in range(ends)]),
                cells,
                lax.ppermute(head, axis, [((i + 1) % count, i) for i in range(ends)]),
            ],
            axis=dim,
        )
    return cells


def neighbour_sum(values, inv_root, neighbours, send_lists):
    rim_width = send_lists.shape[1]
    channels = values.shape[0]
    scaled = values * inv_root
    rim_cells = jnp.concatenate(
        [jnp.take(scaled, send_lists[0], axis=1), jnp.take(scaled, send_lists[1], axis=1)], axis=1
    )
    padded = extended_2(rim_cells.astype(jnp.bfloat16), (("region", 1),), rim_width).astype(
        rim_cells.dtype
    )
    extended = jnp.concatenate(
        [
            scaled,
            padded[:, :rim_width],
            padded[:, 3 * rim_width :],
            jnp.zeros((channels, 1), jnp.float32),
        ],
        axis=1,
    )
    summed = jnp.take(extended, neighbours[0], axis=1)
    for position in range(1, neighbours.shape[0]):
        summed = summed + jnp.take(extended, neighbours[position], axis=1)
    return -inv_root * summed


def chebyshev_basis(start_maps, inv_root, neighbours, send_lists, order):
    terms = [start_maps, neighbour_sum(start_maps, inv_root, neighbours, send_lists)]
    for level in range(2, order):
        terms.append(2.0 * neighbour_sum(terms[-1], inv_root, neighbours, send_lists) - terms[-2])
    return jnp.stack(terms)


def pick_columns(values, columns, usable):
    return jnp.where(
        usable[None, :], jnp.take(values, columns, axis=1), jnp.zeros((), values.dtype)
    )


def body(
    sky_maps, neighbours, send_lists, counts, cheb_weight, first_weight, second_weight, cotangent
):
    pix_count = sky_maps.shape[1]
    rim_width = send_lists.shape[1]
    row_total = cotangent.shape[1]
    order = cheb_weight.shape[0]
    region_size = lax.axis_size("region")
    own_index = lax.axis_index("region")
    capacity = (MOST + region_size - 1) // region_size
    degree = jnp.sum((neighbours < pix_count + 2 * rim_width).astype(jnp.float32), axis=0)
    inv_root = 1.0 / jnp.sqrt(jnp.maximum(degree, 1.0))
    basis = chebyshev_basis(sky_maps.astype(jnp.float32), inv_root, neighbours, send_lists, order)
    rounded = basis.astype(jnp.bfloat16)
    ends = jnp.cumsum(counts)
    starts = ends - counts
    own_pick = jnp.arange(region_size, dtype=jnp.int32) == own_index
    own_start = jnp.sum(jnp.where(own_pick, starts, 0))
    own_count = jnp.sum(jnp.where(own_pick, counts, 0))
    targets = jnp.arange(region_size, dtype=jnp.int32)[:, None]
    place_ids = jnp.arange(capacity, dtype=jnp.int32)[None, :]
    send_row = (place_ids * region_size + jnp.mod(targets - own_start, region_size)).reshape(-1)
    send_fine = send_row < own_count
    send_row = jnp.minimum(send_row, pix_count - 1)
    global_row = jnp.arange(row_total, dtype=jnp.int32) * region_size + own_index
    below = starts[None, :] <= global_row[:, None]
    source = jnp.sum(below.astype(jnp.int32), axis=1) - 1
    source_start = jnp.max(jnp.where(below, starts[None, :], 0), axis=1)
    arrive_col = source * capacity + (global_row - source_start) // region_size
    back_row = place_ids * region_size + jnp.mod(own_index - starts[:, None], region_size)
    back_fine = (back_row < counts[:, None]).reshape(-1)
    back_slot = jnp.minimum((starts[:, None] + back_row) // region_size, row_total - 1).reshape(-1)
    pixel_row = jnp.arange(pix_count, dtype=jnp.int32)
    pixel_fine = pixel_row < own_count
    pixel_col = jnp.minimum(
        jnp.mod(own_start + pixel_row, region_size) * capacity + pixel_row // region_size,
        region_size * capacity - 1,
    )
    weight_part = cheb_weight
    conv_part = lax.psum_scatter(
        jnp.einsum("kco,kcp->op", weight_part, rounded, preferred_element_type=jnp.float32).astype(
            jnp.bfloat16
        ),
        "chan",
        scatter_dimension=0,
        tiled=True,
    )
    outgoing = pick_columns(conv_part, send_row, send_fine)
    incoming = lax.all_to_all(outgoing, "region", split_axis=1, concat_axis=1, tiled=True)
    part_rows = jnp.take(incoming, arrive_col, axis=1)
    features = lax.all_gather(part_rows, "chan", axis=0, tiled=True)
    pre_act = jnp.einsum("fh,fr->hr", first_weight, features, preferred_element_type=jnp.float32)
    gate_val = jax.nn.sigmoid(pre_act)
    hidden = (pre_act * gate_val).astype(jnp.bfloat16)
    weight_part = second_weight
    mlp_out = lax.psum_scatter(
        jnp.einsum("ho,hr->or", weight_part, hidden, preferred_element_type=jnp.float32).astype(
            jnp.bfloat16
        ),
        "chan",
        scatter_dimension=0,
        tiled=True,
    )
    upstream = lax.all_gather(cotangent, "chan", axis=0, tiled=True)
    d_hidden = jnp.einsum("ho,or->hr", second_weight, upstream, preferred_element_type=jnp.float32)
    d_pre = (d_hidden * gate_val * (1.0 + pre_act * (1.0 - gate_val))).astype(jnp.bfloat16)
    second_part = jnp.einsum("hr,or->ho", hidden, upstream, preferred_element_type=jnp.float32)
    first_part = jnp.einsum("fr,hr->fh", features, d_pre, preferred_element_type=jnp.float32)
    weight_part = first_weight
    d_part = lax.psum_scatter(
        jnp.einsum("fh,hr->fr", weight_part, d_pre, preferred_element_type=jnp.float32).astype(
            jnp.bfloat16
        ),
        "chan",
        scatter_dimension=0,
        tiled=True,
    )
    leaving = pick_columns(d_part, back_slot, back_fine)
    arrived = lax.all_to_all(leaving, "region", split_axis=1, concat_axis=1, tiled=True)
    d_pixels_part = pick_columns(arrived, pixel_col, pixel_fine)
    shard_rows = lax.all_gather(d_pixels_part, "chan", axis=0, tiled=True)
    weight_part = cheb_weight
    grad_sum = jnp.einsum(
        "kco,op->kcp", weight_part, shard_rows, preferred_element_type=jnp.float32
    )
    partial_value = jnp.einsum(
        "kcp,op->kco", rounded, shard_rows, preferred_element_type=jnp.float32
    )
    cheb_total, first_total, second_total = lax.psum(
        (partial_value, first_part, second_part), "region"
    )
    grad_scale = 1.0 / math.sqrt(region_size * row_total)
    adjoint = [grad_sum[level] for level in range(order)]
    for level in range(order - 1, 1, -1):
        adjoint[level - 1] = adjoint[level - 1] + 2.0 * neighbour_sum(
            adjoint[level], inv_root, neighbours, send_lists
        )
        adjoint[level - 2] = adjoint[level - 2] - adjoint[level]
    input_grad = adjoint[0] + neighbour_sum(adjoint[1], inv_root, neighbours, send_lists)
    return (
        mlp_out,
        input_grad,
        cheb_total * grad_scale,
        first_total * grad_scale,
        second_total * grad_scale,
    )


def solution(mesh):
    return jax.shard_map(
        body,
        mesh=mesh,
        in_specs=(
            P("chan", "region"),
            P(None, "region"),
            P(None, "region"),
            P(),
            P(None, "chan", None),
            P(None, "chan"),
            P("chan", None),
            P("chan", "region"),
        ),
        out_specs=(
            P("chan", "region"),
            P("chan", "region"),
            P(None, "chan", None),
            P(None, "chan"),
            P("chan", None),
        ),
        check_vma=False,
    )
```

profile of v0, /device:TPU:1, one launch (start us, length us, event | category | flops | bytes accessed | tf_op | source)
XLA Modules:
  0.0 1079.6 jit_solution(8443183412021376778)
XLA Ops:
  9.0 4.9 collective-permute-start
  14.8 5.1 collective-permute-start.1
  25.5 1.0 gather_fusion.11
  26.6 1.0 gather_fusion.10
  27.8 1.0 gather_fusion.9
  28.9 1.0 gather_fusion.8
  30.1 1.0 gather_fusion.7
  31.2 1.0 gather_fusion.6
  32.4 1.0 gather_fusion.5
  33.5 1.0 gather_fusion.4
  36.5 1.9 collective-permute-start.2
  38.5 2.4 collective-permute-start.3
  40.9 2.5 collective-permute-done.3
  43.6 1.0 gather_fusion.21
  44.7 1.0 gather_fusion.20
  45.7 1.0 gather_fusion.19
  46.8 1.0 gather_fusion.18
  47.8 1.0 gather_fusion.17
  48.9 1.0 gather_fusion.16
  51.0 1.0 gather_fusion.14
  54.7 1.9 collective-permute-start.4
  56.7 2.4 collective-permute-start.5
  59.1 2.6 collective-permute-done.5
  62.9 1.0 gather_fusion.30
  65.0 1.0 gather_fusion.28
  73.1 29.8 %reduce-scatter.10.cloned.1.call-done = bf16[32,512]{1,0:T(8,128)(2,1)} async-done(((bf16[128,512]{1,0:T(8,128)(2,1)}), bf16[32,512]{1,0:T(8,128)(2,1)}) %reduce-scatter.10.cloned.1.call-update) | async-done | bytes 32784
  103.8 1.3 gather_fusion.32
  106.0 19.1 %all-to-all-start = ((bf16[32,128,4]{0,2,1:T(4,128)(2,1)}), bf16[32,128,4]{0,2,1:T(4,128)(2,1)S(1)}, u32[]{:S(2)}, u32[]{:S(2)}) async-start(bf16[32,128,4]{0,2,1:T(4,128)(2,1)} %bitcast.48), calls=%async_computation | async-start | bytes 262144 | tf_op jit(solution)/shard_map/all_to_all | solution.py:114
  125.9 9.8 all_gather.10
  135.7 7.0 all-to-all-done
  143.7 9.4 all_gather.9
  155.9 22.9 %reduce-scatter.12.cloned.1.call-done = bf16[32,256]{1,0:T(8,128)(2,1)} async-done(((bf16[128,256]{1,0:T(8,128)(2,1)}), bf16[32,256]{1,0:T(8,128)(2,1)}) %reduce-scatter.12.cloned.1.call-update) | async-done | bytes 16400
  179.7 1.3 gather_fusion.1
  182.0 18.8 %all-to-all-start.1 = ((bf16[32,128,4]{0,2,1:T(4,128)(2,1)}), bf16[32,128,4]{0,2,1:T(4,128)(2,1)S(1)}, u32[]{:S(2)}, u32[]{:S(2)}) async-start(bf16[32,128,4]{0,2,1:T(4,128)(2,1)} %select_select_fusion), calls=%async_computation.2 | async-start | bytes 262144 | tf_op jit(solution)/shard_map/all_to_all | solution.py:144
  201.6 16.6 %all-to-all-done.1 = bf16[32,128,4]{0,2,1:T(4,128)(2,1)S(1)} async-done(((bf16[32,128,4]{0,2,1:T(4,128)(2,1)}), bf16[32,128,4]{0,2,1:T(4,128)(2,1)S(1)}, u32[]{:S(2)}, u32[]{:S(2)}) %all-to-all-start.1) | async-done | bytes 32800 | tf_op jit(solution)/shard_map/all_to_all | solution.py:144
  218.3 1.3 gather_fusion.33
  219.7 9.4 all_gather.11
  231.1 6.4 collective-permute-start.6
  237.5 1.9 collective-permute-start.7
  239.4 485.7 %psum.23 = f32[128,64]{0,1:T(8,128)S(1)} all-reduce(f32[128,64]{0,1:T(8,128)S(1)} %fusion.63), channel_id=1, replica_groups=mesh['region'=128,'chan'=4] {'region'}, use_global_device_ids=true, to_apply=%region_11.15 | all-reduce | flops 8192 | bytes 65536 | tf_op jit(solution)/shard_map/psum | solution.py:154
  736.4 3.6 collective-permute-start.8
  740.0 5.2 collective-permute-start.9
  757.7 1.9 collective-permute-start.10
  759.6 2.4 collective-permute-start.11
  762.7 2.1 collective-permute-done.11
  774.9 276.4 %all-reduce.3.cloned.1.call-done = (f32[4,32,128]{2,1,0:T(8,128)}, f32[128,128]{1,0:T(8,128)}) async-done(((f32[4,32,128]{2,1,0:T(8,128)}, f32[128,128]{1,0:T(8,128)}), (f32[4,32,128]{2,1,0:T(8,128)}, f32[128,128]{1,0:T(8,128)})) %all-reduce.3.cloned.1.call-update) | async-done | bytes 131088 | tf_op jit(solution)/shard_map/psum | solution.py:154
  1051.3 1.5 broadcast_multiply_fusion.1
  1053.5 19.6 %reduce-scatter.8.cloned.1.call-done = bf16[16,256]{1,0:T(8,128)(2,1)} async-done(((bf16[64,256]{1,0:T(8,128)(2,1)}), bf16[16,256]{1,0:T(8,128)(2,1)}) %reduce-scatter.8.cloned.1.call-update) | async-done | bytes 8208 | tf_op jit(solution)/shard_map/reduce_scatter | solution.py:121
  (262 shorter events, 69.3 us)
Async XLA Ops:
  7.2 64.0 %copy-start = (bf16[4,32,128]{2,1,0:T(8,128)(2,1)S(1)}, bf16[4,32,128]{2,1,0:T(8,128)(2,1)}, u32[]{:S(2)}) copy-start(bf16[4,32,128]{2,1,0:T(8,128)(2,1)} %param.18) | copy-start | bytes 98308
  7.2 0.8 copy-start.8
  7.2 0.8 copy-start.1
  7.2 95.8 %reduce-scatter.10.cloned.1.call-start = ((), (), s32[]{:S(2)}) async-start(), calls=%async_computation.6 | async-start | bytes 163840
  9.0 16.3 %collective-permute-start = (bf16[32,128]{1,0:T(8,128)(2,1)S(1)}, bf16[32,128]{1,0:T(8,128)(2,1)S(1)}, u32[]{:S(2)}, u32[]{:S(2)}) collective-permute-start(bf16[32,128]{1,0:T(8,128)(2,1)S(1)} %bitcast_convert_fusion.11), channel_id=1, source_target_pairs={{0,4},{4,8},{8,12},{12,16},{16,20},{20,24},{24,28},{28,32},{32,36}... | collective-permute-start | bytes 24584 | tf_op jit(solution)/shard_map/ppermute | solution.py:19
  14.7 5.2 copy-start.3
  14.8 10.5 collective-permute-start.1
  20.1 0.7 copy-start.7
  36.5 4.4 collective-permute-start.2
  38.5 5.0 collective-permute-start.3
  54.7 4.4 collective-permute-start.4
  56.7 5.0 collective-permute-start.5
  106.0 19.8 %copy-start.6 = (bf16[16,256]{1,0:T(8,128)(2,1)S(1)}, bf16[16,256]{1,0:T(8,128)(2,1)}, u32[]{:S(2)}) copy-start(bf16[16,256]{1,0:T(8,128)(2,1)} %param.21) | copy-start | bytes 24580
  106.0 36.6 %all-to-all-start = ((bf16[32,128,4]{0,2,1:T(4,128)(2,1)}), bf16[32,128,4]{0,2,1:T(4,128)(2,1)S(1)}, u32[]{:S(2)}, u32[]{:S(2)}) async-start(bf16[32,128,4]{0,2,1:T(4,128)(2,1)} %bitcast.48), calls=%async_computation | async-start | bytes 262144 | tf_op jit(solution)/shard_map/all_to_all | solution.py:114
  125.2 53.7 %reduce-scatter.12.cloned.1.call-start = ((), (), s32[]{:S(2)}) async-start(), calls=%async_computation.7 | async-start | bytes 81920
  143.7 9.4 copy-start.4
  153.1 0.7 copy-start.5
  182.0 36.3 %all-to-all-start.1 = ((bf16[32,128,4]{0,2,1:T(4,128)(2,1)}), bf16[32,128,4]{0,2,1:T(4,128)(2,1)S(1)}, u32[]{:S(2)}, u32[]{:S(2)}) async-start(bf16[32,128,4]{0,2,1:T(4,128)(2,1)} %select_select_fusion), calls=%async_computation.2 | async-start | bytes 262144 | tf_op jit(solution)/shard_map/all_to_all | solution.py:144
  200.8 850.5 %all-reduce.3.cloned.1.call-start = ((), (), s32[]{:S(2)}) async-start(), calls=%async_computation.8 | async-start | bytes 262144 | tf_op jit(solution)/shard_map/psum | solution.py:154
  231.1 494.0 %collective-permute-start.6 = (bf16[32,128]{1,0:T(8,128)(2,1)S(1)}, bf16[32,128]{1,0:T(8,128)(2,1)S(1)}, u32[]{:S(2)}, u32[]{:S(2)}) collective-permute-start(bf16[32,128]{1,0:T(8,128)(2,1)S(1)} %bitcast_convert_fusion.5), channel_id=1, source_target_pairs={{0,4},{4,8},{8,12},{12,16},{16,20},{20,24},{24,28},{28,32},{32,36}... | collective-permute-start | bytes 24584 | tf_op jit(solution)/shard_map/ppermute | solution.py:19
  237.5 487.7 %collective-permute-start.7 = (bf16[32,128]{1,0:T(8,128)(2,1)S(1)}, bf16[32,128]{1,0:T(8,128)(2,1)S(1)}, u32[]{:S(2)}, u32[]{:S(2)}) collective-permute-start(bf16[32,128]{1,0:T(8,128)(2,1)S(1)} %bitcast_convert_fusion.4), channel_id=1, source_target_pairs={{4,0},{8,4},{12,8},{16,12},{20,16},{24,20},{28,24},{32,28},{36,32}... | collective-permute-start | bytes 24584 | tf_op jit(solution)/shard_map/ppermute | solution.py:21
  736.4 10.0 collective-permute-start.8
  740.0 6.4 collective-permute-start.9
  746.1 326.9 %reduce-scatter.8.cloned.1.call-start = ((), (), s32[]{:S(2)}) async-start(), calls=%async_computation.5 | async-start | bytes 40960 | tf_op jit(solution)/shard_map/reduce_scatter | solution.py:121
  757.7 5.0 collective-permute-start.10
  759.6 5.1 collective-permute-start.11
  1051.3 1.5 copy-start.2
Sparse Core Ops, SparseCore 0:
  72.3 30.6 reduce-scatter.9
  155.9 22.9 reduce-scatter.11
  746.2 305.0 all-reduce.2
  1054.5 18.4 reduce-scatter.7
where the time goes:
time: 1080 us
  blocking collectives  514 us (48%)
  waiting for transfers between devices  380 us (35%)
  starting transfers between devices  78.5 us (7%)
  local copies, waits for them, and re-layouts  76.8 us (7%)
  between operations  15.1 us (1%)
  other arithmetic  11.6 us (1%)
    psum x1, blocking collectives, body(): lax.psum((partial_value, first_part, second_part), 'region')  486 us
    psum x1, waiting for transfers between devices, body(): lax.psum((partial_value, first_part, second_part), 'region')  276 us
    unnamed x6, waiting for transfers between devices  52.9 us
    gather x84, local copies, waits for them, and re-layouts, neighbour_sum(): summed = summed + jnp.take(extended, neighbours[position], axis=1)  48.1 us
  transfers between devices with their start and end apart: 18, of which 9 were waited for; matrix products, arithmetic and copies ran while one was open for 3% of the time, Pallas kernels for 0%

commit v1 on v0

v1 whole, which is shorter than its diff:
```python
import math

import jax
import jax.numpy as jnp
from jax import lax
from jax.experimental import pallas as pl
from jax.experimental.pallas import tpu as pltpu
from jax.sharding import PartitionSpec as P

F32, BF16, I32 = jnp.float32, jnp.bfloat16, jnp.int32
MESH = pl.DeviceIdType.MESH
PIX, WW, ORDER, GROUP = 512, 128, 4, 32
NZ, NXC, NCHAN, NREGION = 16, 8, 4, 128
TILES = 5
STRIDE = 3
OUT_PART, ROWS_DEV, OUTF = 16, 256, 64

W1, W2, A1, A2, CT, CP, DG, GS, MO, B1, B2, G1, F2, EXCHANGES = range(14)


def dot(left, right, left_dim=1, right_dim=0):
    return lax.dot_general(
        left, right, (((left_dim,), (right_dim,)), ((), ())), preferred_element_type=F32
    )


def iota(shape, dim):
    return lax.broadcasted_iota(I32, shape, dim)


def kernel(
    sky, nb, sl, cnt, cheb, w1, w2, cot,
    mo_out, ig_out, cg_out, fg_out, sg_out,
    amat, smat, mmat, basis, hs, hr, wg1, wg2, s1, r1, s2, r2, cs, ct, cp, cr, dhid,
    dg_s, dg, gs, gr, ms, mr, g1, rg1, hbuf, rg2, ft, rf, fin,
    hsend, hrecv, send, recv, g2send, g2recv, f1send, f1recv,
):
    region, chan = lax.axis_index("region"), lax.axis_index("chan")
    core, z, x = lax.rem(region, 2), lax.rem(lax.div(region, 2), NZ), lax.div(region, 2 * NZ)
    xc = x * 2 + core

    def z_device(zz):
        return ((x * NZ + zz) * 2 + core, chan)

    def z_peer(step):
        other = lax.rem(z + step, NZ)
        return other, z_device(other)

    def xc_peer(step):
        other = lax.rem(xc + step, NXC)
        return other, ((lax.div(other, 2) * NZ + z) * 2 + lax.rem(other, 2), chan)

    def chan_peer(step):
        other = lax.rem(chan + step, NCHAN)
        return other, (region, other)

    lower = (lax.rem(region + NREGION - 1, NREGION), chan)
    upper = (lax.rem(region + 1, NREGION), chan)

    barrier = pltpu.get_barrier_semaphore()

    def greet(peer, count):
        def step(d, carry):
            pl.semaphore_signal(barrier, inc=1, device_id=peer(d)[1], device_id_type=MESH)
            return carry

        lax.fori_loop(1, count, step, 0)

    for device in (lower, upper):
        pl.semaphore_signal(barrier, inc=1, device_id=device, device_id_type=MESH)
    greet(chan_peer, NCHAN)
    greet(xc_peer, NXC)
    greet(z_peer, NZ)

    def spread(key, peer, count, src_at, dst):
        def step(d, carry):
            slot, device = peer(d)
            pltpu.make_async_remote_copy(
                src_ref=src_at(slot), dst_ref=dst, send_sem=send.at[key],
                recv_sem=recv.at[key], device_id=device, device_id_type=MESH,
            ).start()
            return carry

        lax.fori_loop(1, count, step, 0)

    def await_bytes(ref, sem):
        pltpu.make_async_copy(ref, ref, sem).wait()

    links = nb[...]
    inv = 1.0 / jnp.sqrt(
        jnp.maximum(jnp.sum((links != PIX + 2 * WW).astype(F32), axis=0, keepdims=True), 1.0)
    )
    slot_row = iota((PIX, WW), 0)
    for side in range(2):
        smat[:, side * WW : (side + 1) * WW] = (
            jnp.where(slot_row == sl[side : side + 1, :], 1.0, 0.0).astype(BF16)
        )

    def halo_copy(step, side):
        return pltpu.make_async_remote_copy(
            src_ref=hs.at[step, side], dst_ref=hr.at[step, 1 - side],
            send_sem=hsend.at[step, side], recv_sem=hrecv.at[step, 1 - side],
            device_id=(lower, upper)[side], device_id_type=MESH,
        )

    def rim(step, values):
        scaled = values * inv
        high = scaled.astype(BF16)
        edge = dot(high, smat[...]).astype(BF16)
        hs[step, 0] = edge[:, :WW]
        hs[step, 1] = edge[:, WW:]
        return scaled, high

    def halo_start(step):
        for side in range(2):
            halo_copy(step, side).start()

    def inner(pair):
        scaled, high = pair
        low = (scaled - high.astype(F32)).astype(BF16)
        both = dot(jnp.concatenate([high, low], axis=0), amat[:PIX])
        return both[:GROUP] + both[GROUP:]

    def finish(step, local):
        for side in range(2):
            halo_copy(step, 1 - side).wait_recv()
        local = local + dot(hr[step, 0], amat[PIX : PIX + WW])
        local = local + dot(hr[step, 1], amat[PIX + WW :])
        return -inv * local

    v0 = sky[...].astype(F32)
    basis[0:GROUP] = sky[...]
    pair = rim(0, v0)

    pl.semaphore_wait(barrier, 2 + (NCHAN - 1) + (NXC - 1) + (NZ - 1))
    halo_start(0)

    lane, row = iota((NREGION, NREGION), 1), iota((NREGION, NREGION), 0)
    counts = cnt[...].astype(F32)
    zmajor = ((((row & 7) >> 1) * NZ + (row >> 3)) * 2) + (row & 1)
    xcmajor = (((row >> 5) * NZ + (row & 15)) * 2) + ((row >> 4) & 1)
    own_start = jnp.sum(
        jnp.where(lane < region, counts, 0.0), axis=1, keepdims=True
    ).astype(I32)

    def places(order):
        count = jnp.sum(jnp.where(lane == order, counts, 0.0), axis=1, keepdims=True).astype(I32)
        start = jnp.sum(jnp.where(lane < order, counts, 0.0), axis=1, keepdims=True).astype(I32)
        off = (region - start) & (NREGION - 1)
        first = (start + off - region) >> 7
        return count, off, first

    def exchange1(k, key, message):
        s1[k] = message.reshape(NZ, NXC, 128)
        spread(key, z_peer, NZ, lambda slot: s1.at[k, slot], r1.at[k, z])
        r1[k, z] = s1[k, z]

    def exchange2(k, key1, key2):
        await_bytes(r1.at[k, pl.ds(0, NZ - 1)], recv.at[key1])
        for d in range(NXC):
            s2[k, d] = r1[k, :, d, :].astype(BF16)
        spread(key2, xc_peer, NXC, lambda slot: s2.at[k, slot], r2.at[k, xc])
        r2[k, xc] = s2[k, xc]

    def arrived2(k, key2):
        await_bytes(r2.at[k, pl.ds(0, NXC - 1)], recv.at[key2])
        return r2[k].reshape(NREGION, 128).astype(F32).T

    count1, off1, first1 = places(zmajor)
    own_cot = cot[...].astype(F32)
    shifted = [own_cot] + [pltpu.roll(own_cot, ROWS_DEV - s, 1) for s in range(1, 4)]
    shifted = jnp.concatenate(shifted + [jnp.zeros((64, ROWS_DEV), F32)], axis=0).astype(BF16)
    choice = jnp.where(iota((NREGION, ROWS_DEV), 1) == first1, 1.0, 0.0).astype(BF16)
    message = dot(choice, shifted, 1, 1)
    message = jnp.where((lane >> 4) * NREGION + off1 < count1, message, 0.0)
    exchange1(0, A1, message)
    spread(W1, chan_peer, NCHAN, lambda slot: w1, wg1.at[chan])
    spread(W2, chan_peer, NCHAN, lambda slot: w2, wg2.at[chan])

    gone = jnp.where(region == 0, 0, -1)
    gone_up = jnp.where(region == NREGION - 1, 0, -1)
    links = jnp.where((links >= PIX) & (links < PIX + WW) & (gone == 0), PIX + 2 * WW, links)
    links = jnp.where((links >= PIX + WW) & (gone_up == 0), PIX + 2 * WW, links)
    block_row = iota((32, PIX), 0)

    def build(b, carry):
        base = pl.multiple_of(b * 32, 32)
        near = links - base
        total = jnp.zeros((32, PIX), F32)
        for e in range(8):
            total = total + jnp.where(block_row == near[e : e + 1], 1.0, 0.0)
        amat[pl.ds(base, 32), :] = total.astype(BF16)
        return carry

    lax.fori_loop(0, (PIX + 2 * WW) // 32, build, 0)

    v1 = finish(0, inner(pair))
    basis[GROUP : 2 * GROUP] = v1.astype(BF16)
    pair = rim(1, v1)
    halo_start(1)
    local = inner(pair)
    exchange2(0, A1, A2)
    v2 = 2.0 * finish(1, local) - v0
    basis[2 * GROUP : 3 * GROUP] = v2.astype(BF16)
    pair = rim(2, v2)
    halo_start(2)
    local = inner(pair)
    to_pixels = jnp.where(((xcmajor - own_start) & 127) == lane, 1.0, 0.0).astype(BF16)
    columns = dot(arrived2(0, A2).astype(BF16), to_pixels).astype(BF16)
    for s in range(NCHAN):
        cs[s] = columns[s * OUT_PART : (s + 1) * OUT_PART]
    spread(CT, chan_peer, NCHAN, lambda slot: cs.at[slot], ct.at[chan])
    ct[chan] = cs[chan]
    weight = cheb[...]
    weight_t = weight.astype(F32).T.astype(BF16)
    v3 = 2.0 * finish(2, local) - v1
    basis[3 * GROUP :] = v3.astype(BF16)

    part = dot(weight_t, basis[...]).astype(BF16)
    for s in range(NCHAN):
        cp[s] = part[:, s * WW : (s + 1) * WW]
    spread(CP, chan_peer, NCHAN, lambda slot: cp.at[slot], cr.at[chan])
    cr[chan] = cp[chan]

    wg1[chan] = w1[...]
    wg2[chan] = w2[...]
    await_bytes(wg2.at[pl.ds(0, NCHAN - 1)], recv.at[W2])
    await_bytes(wg1.at[pl.ds(0, NCHAN - 1)], recv.at[W1])
    await_bytes(ct.at[pl.ds(0, NCHAN - 1)], recv.at[CT])
    cot_px = ct[...].reshape(OUTF, WW)
    cot_t = cot_px.astype(F32).T.astype(BF16)
    for h in range(NCHAN):
        dhid[h] = dot(cot_t, wg2[h], 1, 1)

    await_bytes(cr.at[pl.ds(0, NCHAN - 1)], recv.at[CP])
    total = cr[0].astype(F32)
    for s in range(1, NCHAN):
        total = total + cr[s].astype(F32)
    features = total.astype(BF16)
    features_t = total.T.astype(BF16)
    hidden, d_pre = [], []
    d_feat = jnp.zeros((WW, 128), F32)
    for h in range(NCHAN):
        pre = dot(features_t, wg1[h])
        gate = jax.nn.sigmoid(pre)
        hidden.append((pre * gate).astype(BF16))
        d_pre.append((dhid[h] * gate * (1.0 + pre * (1.0 - gate))).astype(BF16))
        d_feat = d_feat + dot(d_pre[h], wg1[h], 1, 1)
    dg_s[...] = d_feat.astype(BF16)
    spread(DG, chan_peer, NCHAN, lambda slot: dg_s, dg.at[chan])
    dg[chan] = dg_s[...]

    out_t = jnp.zeros((WW, OUTF), F32)
    for h in range(NCHAN):
        gs[h, 0:128] = dot(features, d_pre[h]).astype(BF16)
        gs[h, 128:192] = dot(cot_px, hidden[h]).astype(BF16)
        out_t = out_t + dot(hidden[h], wg2[h])
    spread(GS, chan_peer, NCHAN, lambda slot: gs.at[slot], gr.at[chan])
    gr[chan] = gs[chan]
    ms[...] = out_t.T.astype(BF16).reshape(NCHAN, OUT_PART, WW)
    spread(MO, chan_peer, NCHAN, lambda slot: ms.at[slot], mr.at[chan])
    mr[chan] = ms[chan]

    await_bytes(dg.at[pl.ds(0, NCHAN - 1)], recv.at[DG])
    d_conv_t = dg[...].reshape(PIX, 128)
    adj3 = dot(weight[3 * GROUP :], d_conv_t, 1, 1)
    pair = rim(3, adj3)
    halo_start(3)
    cheb_part = dot(basis[...], d_conv_t)
    await_bytes(gr.at[pl.ds(0, NCHAN - 1)], recv.at[GS])
    grads = gr[0].astype(F32)
    for s in range(1, NCHAN):
        grads = grads + gr[s].astype(F32)
    g1[:, 0:2] = cheb_part.reshape(NXC, 2, 8, 128)
    g1[:, 2:4] = grads[0:128].reshape(NXC, 2, 8, 128)
    g1[:, 4:5] = grads[128:192].reshape(NXC, 1, 8, 128)
    spread(G1, xc_peer, NXC, lambda slot: g1.at[slot], rg1.at[xc])
    rg1[xc] = g1[xc]
    local = inner(pair)
    d_low = dot(weight[: 3 * GROUP], d_conv_t, 1, 1)
    await_bytes(mr.at[pl.ds(0, NCHAN - 1)], recv.at[MO])
    to_rows = jnp.where(((zmajor - own_start) & 127) == lane, 1.0, 0.0).astype(BF16)
    outs = jnp.concatenate([mr[...].reshape(OUTF, WW), jnp.zeros((64, WW), BF16)], axis=0)
    exchange1(1, B1, dot(to_rows, outs, 1, 1))
    adj2 = d_low[2 * GROUP :] + 2.0 * finish(3, local)
    adj1 = d_low[GROUP : 2 * GROUP] - adj3
    pair = rim(4, adj2)
    halo_start(4)

    await_bytes(rg1.at[pl.ds(0, NXC - 1)], recv.at[G1])
    total = rg1[0]
    for s in range(1, NXC):
        total = total + rg1[s]
    hbuf[...] = total

    def to_owner(j):
        return pltpu.make_async_remote_copy(
            src_ref=hbuf.at[j], dst_ref=rg2.at[z], send_sem=g2send.at[j], recv_sem=g2recv,
            device_id=z_device(j * STRIDE), device_id_type=MESH,
        )

    for j in range(TILES):
        @pl.when(z != j * STRIDE)
        def _(j=j):
            to_owner(j).start()

        @pl.when(z == j * STRIDE)
        def _(j=j):
            rg2[z] = hbuf[j]

    local = inner(pair)
    count2, off2, first2 = places(xcmajor)
    out_row = iota((NREGION, ROWS_DEV), 1)
    for s in range(4):
        fine = (out_row == first2 + s) & (off2 + s * NREGION < count2)
        mmat[s] = jnp.where(fine, 1.0, 0.0).astype(BF16)
    adj1 = adj1 + 2.0 * finish(4, local)
    adj0 = d_low[:GROUP] - adj2
    pair = rim(5, adj1)
    halo_start(5)

    for j in range(TILES):
        @pl.when(z == j * STRIDE)
        def _(j=j):
            await_bytes(rg2.at[pl.ds(0, NZ - 1)], g2recv)
            total = rg2[0]
            for s in range(1, NZ):
                total = total + rg2[s]
            ft[...] = total
            rf[j] = total

            def step(d, carry):
                pltpu.make_async_remote_copy(
                    src_ref=ft, dst_ref=rf.at[j], send_sem=f1send, recv_sem=f1recv.at[j],
                    device_id=z_peer(d)[1], device_id_type=MESH,
                ).start()
                return carry

            lax.fori_loop(1, NZ, step, 0)

    exchange2(1, B1, B2)
    local = inner(pair)
    ig_out[...] = adj0 + finish(5, local)

    for j in range(TILES):
        @pl.when(z != j * STRIDE)
        def _(j=j):
            await_bytes(rf.at[j], f1recv.at[j])
    spread(F2, xc_peer, NXC, lambda slot: rf, fin.at[xc])
    fin[xc] = rf[...]

    rows_t = arrived2(1, B2).astype(BF16)
    result = jnp.zeros((OUT_PART, ROWS_DEV), F32)
    for s in range(4):
        result = result + dot(rows_t[s * OUT_PART : (s + 1) * OUT_PART], mmat[s])
    mo_out[...] = result.astype(BF16)

    scale = 1.0 / math.sqrt(NREGION * ROWS_DEV)
    await_bytes(fin.at[pl.ds(0, NXC - 1)], recv.at[F2])
    cg_out[...] = fin[:, 0:2].reshape(128, 128) * scale
    fg_out[...] = fin[:, 2:4].reshape(128, 128) * scale
    sg_out[...] = (fin[:, 4:5].reshape(64, 128) * scale).T

    for step in range(6):
        for side in range(2):
            halo_copy(step, side).wait_send()
    for key, ref in ((W1, wg1), (W2, wg2), (CT, ct), (CP, cr), (DG, dg), (GS, gr), (MO, mr)):
        await_bytes(ref.at[pl.ds(0, NCHAN - 1)], send.at[key])
    for k, key1, key2 in ((0, A1, A2), (1, B1, B2)):
        await_bytes(r1.at[k, pl.ds(0, NZ - 1)], send.at[key1])
        await_bytes(r2.at[k, pl.ds(0, NXC - 1)], send.at[key2])
    await_bytes(rg1.at[pl.ds(0, NXC - 1)], send.at[G1])
    await_bytes(fin.at[pl.ds(0, NXC - 1)], send.at[F2])
    for j in range(TILES):
        @pl.when(z != j * STRIDE)
        def _(j=j):
            to_owner(j).wait_send()

        @pl.when(z == j * STRIDE)
        def _():
            await_bytes(rg2.at[pl.ds(0, NZ - 1)], f1send)


def body(
    sky_maps, neighbours, send_lists, counts, cheb_weight, first_weight, second_weight, cotangent
):
    dma = pltpu.SemaphoreType.DMA
    vmem = pltpu.VMEM
    scratch = [
        vmem((PIX + 2 * WW, PIX), BF16),
        vmem((PIX, 2 * WW), BF16),
        vmem((4, NREGION, ROWS_DEV), BF16),
        vmem((ORDER * GROUP, PIX), BF16),
        vmem((6, 2, GROUP, WW), BF16),
        vmem((6, 2, GROUP, WW), BF16),
        vmem((NCHAN, 128, 128), BF16),
        vmem((NCHAN, 128, OUTF), BF16),
        vmem((2, NZ, NXC, 128), F32),
        vmem((2, NZ, NXC, 128), F32),
        vmem((2, NXC, NZ, 128), BF16),
        vmem((2, NXC, NZ, 128), BF16),
        vmem((NCHAN, OUT_PART, WW), BF16),
        vmem((NCHAN, OUT_PART, WW), BF16),
        vmem((NCHAN, 128, WW), BF16),
        vmem((NCHAN, 128, WW), BF16),
        vmem((NCHAN, WW, 128), F32),
        vmem((WW, 128), BF16),
        vmem((NCHAN, WW, 128), BF16),
        vmem((NCHAN, 192, 128), BF16),
        vmem((NCHAN, 192, 128), BF16),
        vmem((NCHAN, OUT_PART, WW), BF16),
        vmem((NCHAN, OUT_PART, WW), BF16),
        vmem((NXC, TILES, 8, 128), F32),
        vmem((NXC, TILES, 8, 128), F32),
        vmem((TILES, 8, 128), F32),
        vmem((NZ, 8, 128), F32),
        vmem((8, 128), F32),
        vmem((TILES, 8, 128), F32),
        vmem((NXC, TILES, 8, 128), F32),
        dma((6, 2)),
        dma((6, 2)),
        dma((EXCHANGES,)),
        dma((EXCHANGES,)),
        dma((TILES,)),
        dma,
        dma,
        dma((TILES,)),
    ]
    shape = jax.ShapeDtypeStruct
    mlp_out, input_grad, cheb_grad, first_grad, second_grad = pl.pallas_call(
        kernel,
        out_shape=(
            shape((OUT_PART, ROWS_DEV), BF16),
            shape((GROUP, PIX), F32),
            shape((ORDER * GROUP, 128), F32),
            shape((128, 128), F32),
            shape((128, OUTF), F32),
        ),
        in_specs=[pl.BlockSpec(memory_space=vmem)] * 8,
        out_specs=[pl.BlockSpec(memory_space=vmem)] * 5,
        scratch_shapes=scratch,
        compiler_params=pltpu.CompilerParams(
            collective_id=0, has_side_effects=True, vmem_limit_bytes=40 * 1024 * 1024
        ),
        cost_estimate=pl.CostEstimate(
            flops=600_000_000, bytes_accessed=1_000_000, transcendentals=65_536
        ),
    )(
        sky_maps,
        neighbours,
        send_lists,
        counts.reshape(1, NREGION),
        cheb_weight.reshape(ORDER * GROUP, 128),
        first_weight,
        second_weight,
        cotangent,
    )
    return mlp_out, input_grad, cheb_grad.reshape(ORDER, GROUP, 128), first_grad, second_grad


def solution(mesh):
    return jax.shard_map(
        body,
        mesh=mesh,
        in_specs=(
            P("chan", "region"),
            P(None, "region"),
            P(None, "region"),
            P(),
            P(None, "chan", None),
            P(None, "chan"),
            P("chan", None),
            P("chan", "region"),
        ),
        out_specs=(
            P("chan", "region"),
            P("chan", "region"),
            P(None, "chan", None),
            P(None, "chan"),
            P("chan", None),
        ),
        check_vma=False,
    )
```

time: 1080 us -> 69.2 us (0.06)
  blocking collectives: 514 us -> 0 us
  waiting for transfers between devices: 380 us -> 0 us
  starting transfers between devices: 78.5 us -> 0 us
  local copies, waits for them, and re-layouts: 76.8 us -> 6.25 us
  Pallas kernels: 0 us -> 61.8 us
  between operations: 15.1 us -> 0.72 us
  other arithmetic: 11.6 us -> 0 us
    psum x1 -> x0, blocking collectives: 486 us -> none  [body(): lax.psum((partial_value, first_part, second_part), 'region')]
    psum x1 -> x0, waiting for transfers between devices: 276 us -> none  [body(): lax.psum((partial_value, first_part, second_part), 'region')]
    gather x126 -> x0, local copies, waits for them, and re-layouts: 69.5 us -> none  [the longest x84 48.1 us: neighbour_sum(): summed = summed + jnp.take(extended, neighbours[position], axis=1)]
    pallas_call x0 -> x1, Pallas kernels: none -> 61.8 us  [body(): pl.pallas_call(kernel, out_shape=(shape((OUT_PART, ROWS_DEV), BF16), shap...]
    unnamed x6 -> x0, waiting for transfers between devices: 52.9 us -> none
    ppermute x12 -> x0, starting transfers between devices: 40.2 us -> none  [the longest x6 20.7 us: extended_2(): lax.ppermute(tail, axis, [(i, (i + 1) % count) for i in range(ends)])]
    all_to_all x2 -> x0, starting transfers between devices: 37.9 us -> none  [the longest x1 19.1 us: body(): lax.all_to_all(outgoing, 'region', split_axis=1, concat_axis=1, tiled=True)]
    all_gather x3 -> x0, blocking collectives: 28.6 us -> none  [the longest x1 9.78 us: body(): upstream = lax.all_gather(cotangent, 'chan', axis=0, tiled=True)]
  transfers between devices with their start and end apart: 18 -> 0, of which waited for: 9 -> 0; matrix products, arithmetic and copies ran while one was open for 3% -> 0% of each run, Pallas kernels for 0% -> 0%
where the time goes in v1:
time: 69.2 us; the launch traced here: 68.8 us
  Pallas kernels  61.8 us (89%)
  local copies, waits for them, and re-layouts  6.25 us (9%)
  between operations  0.72 us (1%)
    pallas_call x1, Pallas kernels, body(): pl.pallas_call(kernel, out_shape=(shape((OUT_PART, ROWS_DEV), BF16), shap...  61.8 us
    unnamed x20, local copies, waits for them, and re-layouts  6.25 us

profile of v1, /device:TPU:1, one launch (start us, length us, event | category | flops | bytes accessed | tf_op | source)
XLA Modules:
  0.0 68.8 jit_solution(2794019669047261047)
XLA Ops:
  0.6 0.0 copy-start
  0.6 0.0 copy-start.3
  0.7 0.0 copy-start.5
  0.7 0.0 copy-start.6
  0.7 0.8 %copy.13.w2 = bf16[128,64]{1,0:T(8,128)(2,1)S(1)} copy(bf16[128,64]{0,1:T(8,128)(2,1)} %param.14) | data formatting | bytes 32768 | tf_op args[6]
  1.5 0.0 copy-done
  1.5 0.0 copy-done.3
  1.5 0.0 copy-done.5
  1.6 0.0 copy-done.6
  1.6 0.0 copy-start.1
  1.6 0.7 %copy-done.1 = bf16[4,32,128]{2,1,0:T(8,128)(2,1)S(1)} copy-done((bf16[4,32,128]{2,1,0:T(8,128)(2,1)S(1)}, bf16[4,32,128]{2,1,0:T(8,128)(2,1)}, u32[]{:S(2)}) %copy-start.1) | copy-done | bytes 32792
  2.3 0.0 copy-start.2
  2.3 0.8 %copy-done.2 = bf16[128,128]{1,0:T(8,128)(2,1)S(1)} copy-done((bf16[128,128]{1,0:T(8,128)(2,1)S(1)}, bf16[128,128]{1,0:T(8,128)(2,1)}, u32[]{:S(2)}) %copy-start.2) | copy-done | bytes 32792
  3.1 0.0 copy-start.4
  3.1 0.7 %copy-done.4 = bf16[16,256]{1,0:T(8,128)(2,1)S(1)} copy-done((bf16[16,256]{1,0:T(8,128)(2,1)S(1)}, bf16[16,256]{1,0:T(8,128)(2,1)}, u32[]{:S(2)}) %copy-start.4) | copy-done | bytes 8216
  3.8 61.8 %shard_map.119 = (bf16[16,256]{1,0:T(8,128)(2,1)S(1)}, f32[32,512]{1,0:T(8,128)S(1)}, f32[128,128]{1,0:T(8,128)S(1)}, f32[128,128]{1,0:T(8,128)S(1)}, f32[128,64]{1,0:T(8,128)S(1)}) custom-call(bf16[32,512]{1,0:T(8,128)(2,1)S(1)} %copy-done, s32[8,512]{1,0:T(8,128)S(1)} %copy-done.3, s32[2,128]{1,0:T(2,128)S(1)} %copy-done.5, s32[1,128]{1,0:T(1,128)S(1)} %bitcast.5, ...), custom_call_target="tpu_custom_call" | custom-call | flops 600000000 | bytes 1000000 | tf_op jit(solution)/shard_map/pallas_call | solution.py:430
  65.6 0.7 %copy.14 = f32[128,64]{0,1:T(8,128)} copy(f32[128,64]{1,0:T(8,128)S(1)} %get-tuple-element.19) | data formatting | bytes 65536
  66.3 0.6 copy.19
  66.9 0.6 copy.20
  67.5 0.6 copy.21
  68.2 0.6 copy.22
Async XLA Ops:
  0.6 0.9 %copy-start = (bf16[32,512]{1,0:T(8,128)(2,1)S(1)}, bf16[32,512]{1,0:T(8,128)(2,1)}, u32[]{:S(2)}) copy-start(bf16[32,512]{1,0:T(8,128)(2,1)} %sky.1) | copy-start | bytes 98308
  0.6 0.9 %copy-start.3 = (s32[8,512]{1,0:T(8,128)S(1)}, s32[8,512]{1,0:T(8,128)}, u32[]{:S(2)}) copy-start(s32[8,512]{1,0:T(8,128)} %nb.1) | copy-start | bytes 49156
  0.7 0.9 %copy-start.5 = (s32[2,128]{1,0:T(2,128)S(1)}, s32[2,128]{1,0:T(2,128)}, u32[]{:S(2)}) copy-start(s32[2,128]{1,0:T(2,128)} %sl.1) | copy-start | bytes 3076
  0.7 0.9 %copy-start.6 = (s32[128]{0:T(128)S(1)}, s32[128]{0:T(128)}, u32[]{:S(2)}) copy-start(s32[128]{0:T(128)} %param.11) | copy-start | bytes 1540
  1.6 0.8 %copy-start.1 = (bf16[4,32,128]{2,1,0:T(8,128)(2,1)S(1)}, bf16[4,32,128]{2,1,0:T(8,128)(2,1)}, u32[]{:S(2)}) copy-start(bf16[4,32,128]{2,1,0:T(8,128)(2,1)} %param.12) | copy-start | bytes 98308
  2.3 0.8 %copy-start.2 = (bf16[128,128]{1,0:T(8,128)(2,1)S(1)}, bf16[128,128]{1,0:T(8,128)(2,1)}, u32[]{:S(2)}) copy-start(bf16[128,128]{1,0:T(8,128)(2,1)} %w1.1) | copy-start | bytes 98308
  3.1 0.7 %copy-start.4 = (bf16[16,256]{1,0:T(8,128)(2,1)S(1)}, bf16[16,256]{1,0:T(8,128)(2,1)}, u32[]{:S(2)}) copy-start(bf16[16,256]{1,0:T(8,128)(2,1)} %cot.1) | copy-start | bytes 24580

commit v2 on v1

v2 whole, which is shorter than its diff:
```python
import math

import jax
import jax.numpy as jnp
from jax import lax
from jax.experimental import pallas as pl
from jax.experimental.pallas import tpu as pltpu
from jax.sharding import PartitionSpec as P

F32, BF16, I32 = jnp.float32, jnp.bfloat16, jnp.int32
MESH = pl.DeviceIdType.MESH
PIX, WW, ORDER, GROUP = 512, 128, 4, 32
NZ, NX, NXC, NCHAN, NREGION = 16, 4, 8, 4, 128
NPLANE = NXC * NCHAN
PIECE, CORE1 = 48, 32
OUT_PART, ROWS_DEV, OUTF = 16, 256, 64

W1, W2, A1, A2, CP, DG, GS, B1, B2, G1, G2, F2, EXCHANGES = range(13)


def dot(left, right, left_dim=1, right_dim=0):
    return lax.dot_general(
        left, right, (((left_dim,), (right_dim,)), ((), ())), preferred_element_type=F32
    )


def iota(shape, dim):
    return lax.broadcasted_iota(I32, shape, dim)


def kernel(
    sky_in, nb_in, sl_in, cnt_in, cheb_in, w1_in, w2_in, cot_in,
    mo_out, ig_out, cg_out, fg_out, sg_out,
    sky, nb, sl, cnt, cheb, w1, w2, cot,
    amat, smat, mmat, emat, basis, hs, hr, wg1, wg2, s1, r1, s2, r2, cp, cr, dhid,
    dg_s, dg, gs, gr, g1, rg1, hbuf, rg2, ft, fin,
    loads, hsend, hrecv, send, recv,
):
    region, chan = lax.axis_index("region"), lax.axis_index("chan")
    core, z, x = lax.rem(region, 2), lax.rem(lax.div(region, 2), NZ), lax.div(region, 2 * NZ)
    xc = x * 2 + core

    plane = xc * NCHAN + chan

    def z_peer(step):
        other = lax.rem(z + step, NZ)
        return other, ((x * NZ + other) * 2 + core, chan)

    def plane_peer(step):
        other = lax.rem(plane + step, NPLANE)
        there = lax.div(other, NCHAN)
        there = (lax.div(there, 2) * NZ + z) * 2 + lax.rem(there, 2)
        return other, (there, lax.rem(other, NCHAN))

    def xc_peer(step):
        other = lax.rem(xc + step, NXC)
        return other, ((lax.div(other, 2) * NZ + z) * 2 + lax.rem(other, 2), chan)

    def chan_peer(step):
        other = lax.rem(chan + step, NCHAN)
        return other, (region, other)

    lower = (lax.rem(region + NREGION - 1, NREGION), chan)
    upper = (lax.rem(region + 1, NREGION), chan)

    barrier = pltpu.get_barrier_semaphore()

    def greet(peer, count):
        def step(d, carry):
            pl.semaphore_signal(barrier, inc=1, device_id=peer(d)[1], device_id_type=MESH)
            return carry

        lax.fori_loop(1, count, step, 0)

    greet(z_peer, NZ)
    for device in (lower, upper):
        pl.semaphore_signal(barrier, inc=1, device_id=device, device_id_type=MESH)
    greet(plane_peer, NPLANE)

    pairs = (
        (nb_in, nb), (sl_in, sl), (sky_in, sky), (cnt_in, cnt),
        (cot_in, cot), (w1_in, w1), (w2_in, w2), (cheb_in, cheb),
    )
    load = {id(there): pltpu.make_async_copy(here, there, loads.at[i]) for i, (here, there) in enumerate(pairs)}
    for copy in load.values():
        copy.start()

    def loaded(*refs):
        for ref in refs:
            load[id(ref)].wait()

    def spread(key, peer, count, src_at, dst):
        def step(d, carry):
            slot, device = peer(d)
            pltpu.make_async_remote_copy(
                src_ref=src_at(slot), dst_ref=dst, send_sem=send.at[key],
                recv_sem=recv.at[key], device_id=device, device_id_type=MESH,
            ).start()
            return carry

        lax.fori_loop(1, count, step, 0)

    def await_bytes(ref, sem):
        pltpu.make_async_copy(ref, ref, sem).wait()

    loaded(nb, sl, sky)
    links = nb[...]
    inv = 1.0 / jnp.sqrt(
        jnp.maximum(jnp.sum((links != PIX + 2 * WW).astype(F32), axis=0, keepdims=True), 1.0)
    )
    slot_row = iota((PIX, WW), 0)
    for side in range(2):
        smat[:, side * WW : (side + 1) * WW] = (
            jnp.where(slot_row == sl[side : side + 1, :], 1.0, 0.0).astype(BF16)
        )

    def halo_copy(step, side):
        return pltpu.make_async_remote_copy(
            src_ref=hs.at[step, side], dst_ref=hr.at[step, 1 - side],
            send_sem=hsend.at[step, side], recv_sem=hrecv.at[step, 1 - side],
            device_id=(lower, upper)[side], device_id_type=MESH,
        )

    def rim(step, values):
        scaled = values * inv
        high = scaled.astype(BF16)
        edge = dot(high, smat[...]).astype(BF16)
        hs[step, 0] = edge[:, :WW]
        hs[step, 1] = edge[:, WW:]
        return scaled, high

    def halo_start(step):
        for side in range(2):
            halo_copy(step, side).start()

    def inner(pair):
        scaled, high = pair
        low = (scaled - high.astype(F32)).astype(BF16)
        both = dot(jnp.concatenate([high, low], axis=0), amat[:PIX])
        return both[:GROUP] + both[GROUP:]

    def finish(step, local):
        for side in range(2):
            halo_copy(step, 1 - side).wait_recv()
        local = local + dot(hr[step, 0], amat[PIX : PIX + WW])
        local = local + dot(hr[step, 1], amat[PIX + WW :])
        return -inv * local

    v0 = sky[...].astype(F32)
    basis[0:GROUP] = sky[...]
    pair = rim(0, v0)

    pl.semaphore_wait(barrier, 2 + (NPLANE - 1) + (NZ - 1))
    halo_start(0)

    loaded(cnt, cot)
    counts = cnt[...].astype(F32)
    own_start = jnp.sum(
        jnp.where(iota((64, NREGION), 1) < region, counts, 0.0), axis=1, keepdims=True
    )[:1].astype(I32)

    def places(order):
        lane = iota(order.shape, 1)
        count = jnp.sum(jnp.where(lane == order, counts, 0.0), axis=1, keepdims=True).astype(I32)
        start = jnp.sum(jnp.where(lane < order, counts, 0.0), axis=1, keepdims=True).astype(I32)
        off = (region - start) & (NREGION - 1)
        first = (start + off - region) >> 7
        return count, off, first

    def exchange1(k, key, message):
        s1[k] = message.reshape(NZ, NX, 128)
        spread(key, z_peer, NZ, lambda slot: s1.at[k, slot], r1.at[k, z])
        r1[k, z] = s1[k, z]

    def exchange2(k, key1, key2):
        await_bytes(r1.at[k, pl.ds(0, NZ - 1)], recv.at[key1])
        here = jnp.concatenate([r1[k, :, i, :] for i in range(NX)], axis=0).astype(BF16)
        moved = dot(here, emat[...]).astype(BF16)
        for i in range(NX):
            for b in range(2 * NCHAN):
                s2[k, i * 2 * NCHAN + b] = moved[i * NZ : (i + 1) * NZ, b * 128 : (b + 1) * 128]
        spread(key2, plane_peer, NPLANE, lambda slot: s2.at[k, slot], r2.at[k, plane])
        r2[k, plane] = s2[k, plane]

    def arrived2(k, key2):
        await_bytes(r2.at[k, pl.ds(0, NPLANE - 1)], recv.at[key2])
        parts = r2[k].astype(F32).reshape(NXC, NCHAN, NZ, 128)
        total = parts[:, 0]
        for s in range(1, NCHAN):
            total = total + parts[:, s]
        return total.reshape(NREGION, 128).T.astype(BF16)

    pair_row = iota((NZ * NX, NREGION), 0)
    zmajor = ((pair_row & 3) * NZ + (pair_row >> 2)) * 2
    count0, off0, first0 = places(zmajor)
    count1, off1, first1 = places(zmajor + 1)
    own_cot = cot[...].astype(F32)
    shifted = [own_cot] + [pltpu.roll(own_cot, ROWS_DEV - s, 1) for s in range(1, 4)]
    shifted = jnp.concatenate(shifted, axis=0).astype(BF16)
    empty = jnp.zeros_like(shifted)
    shifted = jnp.concatenate(
        [jnp.concatenate([shifted, empty], axis=1), jnp.concatenate([empty, shifted], axis=1)], axis=0
    )
    own_row = iota((NZ * NX, ROWS_DEV), 1)
    choice = jnp.concatenate([own_row == first0, own_row == first1], axis=1)
    message = dot(jnp.where(choice, 1.0, 0.0).astype(BF16), shifted, 1, 1)
    lane64 = iota((NZ * NX, NREGION), 1)
    room = jnp.where(lane64 < 64, count0 - off0, count1 - off1)
    message = jnp.where(((lane64 & 63) >> 4) * NREGION < room, message, 0.0)
    exchange1(0, A1, message)
    loaded(w1, w2)
    spread(W1, chan_peer, NCHAN, lambda slot: w1, wg1.at[chan])
    spread(W2, chan_peer, NCHAN, lambda slot: w2, wg2.at[chan])

    from_row, to_lane = iota((128, 1024), 0), iota((128, 1024), 1)
    emat[...] = jnp.where(
        ((from_row >> 4) == (to_lane >> 7))
        & ((to_lane & 127) == chan * OUT_PART + (from_row & 15)),
        1.0, 0.0,
    ).astype(BF16)

    gone = jnp.where(region == 0, 0, -1)
    gone_up = jnp.where(region == NREGION - 1, 0, -1)
    links = jnp.where((links >= PIX) & (links < PIX + WW) & (gone == 0), PIX + 2 * WW, links)
    links = jnp.where((links >= PIX + WW) & (gone_up == 0), PIX + 2 * WW, links)
    block_row = iota((32, PIX), 0)

    def build(b, carry):
        base = pl.multiple_of(b * 32, 32)
        near = links - base
        total = jnp.zeros((32, PIX), F32)
        for e in range(8):
            total = total + jnp.where(block_row == near[e : e + 1], 1.0, 0.0)
        amat[pl.ds(base, 32), :] = total.astype(BF16)
        return carry

    lax.fori_loop(0, (PIX + 2 * WW) // 32, build, 0)

    v1 = finish(0, inner(pair))
    basis[GROUP : 2 * GROUP] = v1.astype(BF16)
    pair = rim(1, v1)
    halo_start(1)
    local = inner(pair)
    v2 = 2.0 * finish(1, local) - v0
    basis[2 * GROUP : 3 * GROUP] = v2.astype(BF16)
    pair = rim(2, v2)
    halo_start(2)
    local = inner(pair)
    exchange2(0, A1, A2)
    lane, row = iota((NREGION, NREGION), 1), iota((NREGION, NREGION), 0)
    xcmajor = (((row >> 5) * NZ + (row & 15)) * 2) + ((row >> 4) & 1)
    to_pixels = jnp.where(((xcmajor - own_start) & 127) == lane, 1.0, 0.0).astype(BF16)
    loaded(cheb)
    weight = cheb[...]
    weight_t = weight.astype(F32).T.astype(BF16)
    v3 = 2.0 * finish(2, local) - v1
    basis[3 * GROUP :] = v3.astype(BF16)

    part = dot(weight_t, basis[...]).astype(BF16)
    for s in range(NCHAN):
        cp[s] = part[:, s * WW : (s + 1) * WW]
    spread(CP, chan_peer, NCHAN, lambda slot: cp.at[slot], cr.at[chan])
    cr[chan] = cp[chan]

    wg1[chan] = w1[...]
    wg2[chan] = w2[...]
    await_bytes(wg2.at[pl.ds(0, NCHAN - 1)], recv.at[W2])
    await_bytes(wg1.at[pl.ds(0, NCHAN - 1)], recv.at[W1])
    columns = dot(arrived2(0, A2), to_pixels)[:OUTF]
    cot_px = columns.astype(BF16)
    cot_t = columns.T.astype(BF16)
    for h in range(NCHAN):
        dhid[h] = dot(cot_t, wg2[h])

    await_bytes(cr.at[pl.ds(0, NCHAN - 1)], recv.at[CP])
    total = cr[0].astype(F32)
    for s in range(1, NCHAN):
        total = total + cr[s].astype(F32)
    features = total.astype(BF16)
    features_t = total.T.astype(BF16)
    hidden, d_pre = [], []
    d_feat = jnp.zeros((WW, 128), F32)
    for h in range(NCHAN):
        pre = dot(features_t, wg1[h])
        gate = jax.nn.sigmoid(pre)
        hidden.append((pre * gate).astype(BF16))
        d_pre.append((dhid[h] * gate * (1.0 + pre * (1.0 - gate))).astype(BF16))
        d_feat = d_feat + dot(d_pre[h], wg1[h], 1, 1)
    dg_s[...] = d_feat.astype(BF16)
    spread(DG, chan_peer, NCHAN, lambda slot: dg_s, dg.at[chan])
    dg[chan] = dg_s[...]

    out_t = jnp.zeros((WW, OUTF), F32)
    for h in range(NCHAN):
        gs[h, 0:128] = dot(features, d_pre[h]).astype(BF16)
        gs[h, 128:192] = dot(cot_px, hidden[h]).astype(BF16)
        out_t = out_t + dot(hidden[h], wg2[h], 1, 1)
    spread(GS, chan_peer, NCHAN, lambda slot: gs.at[slot], gr.at[chan])
    gr[chan] = gs[chan]
    outs = out_t.T.astype(BF16)
    empty = jnp.zeros_like(outs)
    outs = jnp.concatenate(
        [jnp.concatenate([outs, empty], axis=1), jnp.concatenate([empty, outs], axis=1)], axis=0
    )
    to_rows = jnp.concatenate(
        [((zmajor + i - own_start) & 127) == lane64 for i in range(2)], axis=1
    )
    exchange1(1, B1, dot(jnp.where(to_rows, 1.0, 0.0).astype(BF16), outs, 1, 1))

    await_bytes(dg.at[pl.ds(0, NCHAN - 1)], recv.at[DG])
    d_conv_t = dg[...].reshape(PIX, 128)
    adj3 = dot(weight[3 * GROUP :], d_conv_t, 1, 1)
    pair = rim(3, adj3)
    halo_start(3)
    cheb_part = dot(basis[...], d_conv_t)
    await_bytes(gr.at[pl.ds(0, NCHAN - 1)], recv.at[GS])
    grads = gr[0].astype(F32)
    for s in range(1, NCHAN):
        grads = grads + gr[s].astype(F32)
    g1[:, 0:16] = cheb_part.astype(BF16).reshape(NXC, 16, 128)
    g1[:, 16:32] = grads[0:128].astype(BF16).reshape(NXC, 16, 128)
    for i in range(NX):
        g1[2 * i, 32:48] = grads[128 + 16 * i : 144 + 16 * i].astype(BF16)
        g1[2 * i + 1, 32:48] = jnp.zeros((16, 128), BF16)
    spread(G1, xc_peer, NXC, lambda slot: g1.at[slot], rg1.at[xc])
    rg1[xc] = g1[xc]
    local = inner(pair)
    d_low = dot(weight[: 3 * GROUP], d_conv_t, 1, 1)
    adj2 = d_low[2 * GROUP :] + 2.0 * finish(3, local)
    adj1 = d_low[GROUP : 2 * GROUP] - adj3
    pair = rim(4, adj2)
    halo_start(4)

    await_bytes(rg1.at[pl.ds(0, NXC - 1)], recv.at[G1])
    total = rg1[0].astype(F32)
    for s in range(1, NXC):
        total = total + rg1[s].astype(F32)
    hbuf[...] = total.astype(BF16)
    for own_core, rows in ((0, PIECE), (1, CORE1)):
        @pl.when(core == own_core)
        def _(rows=rows):
            spread(G2, z_peer, NZ, lambda slot: hbuf.at[pl.ds(0, rows)], rg2.at[z, pl.ds(0, rows)])

    rg2[z] = hbuf[...]
    exchange2(1, B1, B2)
    local = inner(pair)
    count2, off2, first2 = places(xcmajor)
    out_row = iota((NREGION, ROWS_DEV), 1)
    for s in range(4):
        fine = (out_row == first2 + s) & (off2 + s * NREGION < count2)
        mmat[s] = jnp.where(fine, 1.0, 0.0).astype(BF16)
    adj1 = adj1 + 2.0 * finish(4, local)
    adj0 = d_low[:GROUP] - adj2
    pair = rim(5, adj1)
    halo_start(5)

    local = inner(pair)
    ig_out[...] = adj0 + finish(5, local)

    for own_core, rows in ((0, PIECE), (1, CORE1)):
        @pl.when(core == own_core)
        def _(rows=rows):
            await_bytes(rg2.at[pl.ds(0, NZ - 1), pl.ds(0, rows)], recv.at[G2])
            total = rg2[0, 0:rows].astype(F32)
            for s in range(1, NZ):
                total = total + rg2[s, 0:rows].astype(F32)
            ft[0:rows] = total.astype(BF16)
            if rows < PIECE:
                ft[rows:] = jnp.zeros((PIECE - rows, 128), BF16)

    spread(F2, xc_peer, NXC, lambda slot: ft, fin.at[xc])
    fin[xc] = ft[...]

    rows_t = arrived2(1, B2)
    result = jnp.zeros((OUT_PART, ROWS_DEV), F32)
    for s in range(4):
        result = result + dot(rows_t[s * OUT_PART : (s + 1) * OUT_PART], mmat[s])
    mo_out[...] = result.astype(BF16)

    scale = 1.0 / math.sqrt(NREGION * ROWS_DEV)
    await_bytes(fin.at[pl.ds(0, NXC - 1)], recv.at[F2])
    cg_out[...] = fin[:, 0:16].astype(F32).reshape(128, 128) * scale
    fg_out[...] = fin[:, 16:32].astype(F32).reshape(128, 128) * scale
    for i in range(NX):
        sg_out[16 * i : 16 * (i + 1)] = fin[2 * i, 32:48].astype(F32) * scale

    for step in range(6):
        for side in range(2):
            halo_copy(step, side).wait_send()
    for key, ref in ((W1, wg1), (W2, wg2), (CP, cr), (DG, dg), (GS, gr)):
        await_bytes(ref.at[pl.ds(0, NCHAN - 1)], send.at[key])
    for k, key1, key2 in ((0, A1, A2), (1, B1, B2)):
        await_bytes(r1.at[k, pl.ds(0, NZ - 1)], send.at[key1])
        await_bytes(r2.at[k, pl.ds(0, NPLANE - 1)], send.at[key2])
    await_bytes(rg1.at[pl.ds(0, NXC - 1)], send.at[G1])
    await_bytes(fin.at[pl.ds(0, NXC - 1)], send.at[F2])
    for own_core, rows in ((0, PIECE), (1, CORE1)):
        @pl.when(core == own_core)
        def _(rows=rows):
            await_bytes(rg2.at[pl.ds(0, NZ - 1), pl.ds(0, rows)], send.at[G2])


def writer(*refs):
    count = len(refs) // 2
    sems = refs[-1]
    copies = [pltpu.make_async_copy(refs[i], refs[count + i], sems.at[i]) for i in range(count)]
    for copy in copies:
        copy.start()
    for copy in copies:
        copy.wait()


def body(
    sky_maps, neighbours, send_lists, counts, cheb_weight, first_weight, second_weight, cotangent
):
    dma = pltpu.SemaphoreType.DMA
    vmem = pltpu.VMEM
    shape = jax.ShapeDtypeStruct
    args = (
        sky_maps,
        neighbours,
        send_lists,
        counts.reshape(1, NREGION),
        cheb_weight.reshape(ORDER * GROUP, 128),
        first_weight,
        second_weight.T,
        cotangent,
    )
    scratch = [vmem(arg.shape, arg.dtype) for arg in args] + [
        vmem((PIX + 2 * WW, PIX), BF16),
        vmem((PIX, 2 * WW), BF16),
        vmem((4, NREGION, ROWS_DEV), BF16),
        vmem((128, 1024), BF16),
        vmem((ORDER * GROUP, PIX), BF16),
        vmem((6, 2, GROUP, WW), BF16),
        vmem((6, 2, GROUP, WW), BF16),
        vmem((NCHAN, 128, 128), BF16),
        vmem((NCHAN, OUTF, 128), BF16),
        vmem((2, NZ, NX, 128), F32),
        vmem((2, NZ, NX, 128), F32),
        vmem((2, NPLANE, NZ, 128), BF16),
        vmem((2, NPLANE, NZ, 128), BF16),
        vmem((NCHAN, 128, WW), BF16),
        vmem((NCHAN, 128, WW), BF16),
        vmem((NCHAN, WW, 128), F32),
        vmem((WW, 128), BF16),
        vmem((NCHAN, WW, 128), BF16),
        vmem((NCHAN, 192, 128), BF16),
        vmem((NCHAN, 192, 128), BF16),
        vmem((NXC, PIECE, 128), BF16),
        vmem((NXC, PIECE, 128), BF16),
        vmem((PIECE, 128), BF16),
        vmem((NZ, PIECE, 128), BF16),
        vmem((PIECE, 128), BF16),
        vmem((NXC, PIECE, 128), BF16),
        dma((8,)),
        dma((6, 2)),
        dma((6, 2)),
        dma((EXCHANGES,)),
        dma((EXCHANGES,)),
    ]
    results = (
        shape((OUT_PART, ROWS_DEV), BF16),
        shape((GROUP, PIX), F32),
        shape((ORDER * GROUP, 128), F32),
        shape((128, 128), F32),
        shape((OUTF, 128), F32),
    )
    found = pl.pallas_call(
        kernel,
        out_shape=results,
        in_specs=[pl.BlockSpec(memory_space=pl.ANY)] * 8,
        out_specs=[pl.BlockSpec(memory_space=vmem)] * 5,
        scratch_shapes=scratch,
        compiler_params=pltpu.CompilerParams(
            collective_id=0, has_side_effects=True, vmem_limit_bytes=60 * 1024 * 1024
        ),
        cost_estimate=pl.CostEstimate(
            flops=600_000_000, bytes_accessed=1_000_000, transcendentals=65_536
        ),
    )(*args)
    mlp_out, input_grad, cheb_grad, first_grad, second_grad = pl.pallas_call(
        writer,
        out_shape=results,
        in_specs=[pl.BlockSpec(memory_space=pl.ANY)] * 5,
        out_specs=[pl.BlockSpec(memory_space=pl.ANY)] * 5,
        scratch_shapes=[dma((5,))],
    )(*found)
    return mlp_out, input_grad, cheb_grad.reshape(ORDER, GROUP, 128), first_grad, second_grad.T


def solution(mesh):
    return jax.shard_map(
        body,
        mesh=mesh,
        in_specs=(
            P("chan", "region"),
            P(None, "region"),
            P(None, "region"),
            P(),
            P(None, "chan", None),
            P(None, "chan"),
            P("chan", None),
            P("chan", "region"),
        ),
        out_specs=(
            P("chan", "region"),
            P("chan", "region"),
            P(None, "chan", None),
            P(None, "chan"),
            P("chan", None),
        ),
        check_vma=False,
    )
```

time: 69.2 us -> 69.7 us (level)
  Pallas kernels: 61.8 us -> 68.8 us
  local copies, waits for them, and re-layouts: 6.25 us -> 0 us
    pallas_call x1 -> x2, Pallas kernels: 61.8 us -> 68.8 us  [the longest x1 60.5 us: body(): pl.pallas_call(kernel, out_shape=results, in_specs=[pl.BlockSpec(memory_s...]
    unnamed x20 -> x0, local copies, waits for them, and re-layouts: 6.25 us -> none
where the time goes in v2:
time: 69.7 us; the launch traced here: 69.5 us
  Pallas kernels  68.8 us (99%)
    pallas_call x1, Pallas kernels, body(): pl.pallas_call(kernel, out_shape=results, in_specs=[pl.BlockSpec(memory_s...  60.5 us
    pallas_call x1, Pallas kernels, body(): pl.pallas_call(writer, out_shape=results, in_specs=[pl.BlockSpec(memory_s...  8.35 us

profile of v2, /device:TPU:1, one launch (start us, length us, event | category | flops | bytes accessed | tf_op | source)
XLA Modules:
  0.0 69.5 jit_solution(12102956940536302084)
XLA Ops:
  0.6 60.5 %shard_map.119 = (bf16[16,256]{1,0:T(8,128)(2,1)}, f32[32,512]{1,0:T(8,128)}, f32[128,128]{1,0:T(8,128)}, f32[128,128]{1,0:T(8,128)}, f32[64,128]{1,0:T(8,128)}) custom-call(bf16[32,512]{1,0:T(8,128)(2,1)} %sky_in.1, s32[8,512]{1,0:T(8,128)} %nb_in.1, s32[2,128]{1,0:T(2,128)} %sl_in.1, s32[1,128]{1,0:T(1,128)} %bitcast.9, bf16[128,128]{1,0:T(8,128)(2,1)} %bitcast.6, ...), custom_call_target="tpu_custom_call" | custom-call | flops 600000000 | bytes 1000000 | tf_op jit(solution)/shard_map/pallas_call | solution.py:469
  61.1 8.3 %shard_map.120 = (bf16[16,256]{1,0:T(8,128)(2,1)}, f32[32,512]{1,0:T(8,128)}, f32[128,128]{1,0:T(8,128)}, f32[128,128]{1,0:T(8,128)}, f32[64,128]{1,0:T(8,128)}) custom-call(bf16[16,256]{1,0:T(8,128)(2,1)} %get-tuple-element.15.refs_0_, f32[32,512]{1,0:T(8,128)} %get-tuple-element.16.refs_1_, f32[128,128]{1,0:T(8,128)} %get-tuple-element.17.refs_2_, ...), custom_call_target="tpu_custom_call" | custom-call | tf_op jit(solution)/shard_map/pallas_call | solution.py:482

commit v3 on v2

--- a/solution.py
+++ b/solution.py
@@ -12,10 +12,10 @@
 PIX, WW, ORDER, GROUP = 512, 128, 4, 32
 NZ, NX, NXC, NCHAN, NREGION = 16, 4, 8, 4, 128
 NPLANE = NXC * NCHAN
-PIECE, CORE1 = 48, 32
+NDUO, TILE = 16, 16
 OUT_PART, ROWS_DEV, OUTF = 16, 256, 64
 
-W1, W2, A1, A2, CP, DG, GS, B1, B2, G1, G2, F2, EXCHANGES = range(13)
+W1, W2, A1, A2, CP, DG, GS, B1, B2, G1, G2, F2, H1, H2, I2, EXCHANGES = range(16)
 
 
 def dot(left, right, left_dim=1, right_dim=0):
@@ -33,8 +33,8 @@
     mo_out, ig_out, cg_out, fg_out, sg_out,
     sky, nb, sl, cnt, cheb, w1, w2, cot,
     amat, smat, mmat, emat, basis, hs, hr, wg1, wg2, s1, r1, s2, r2, cp, cr, dhid,
-    dg_s, dg, gs, gr, g1, rg1, hbuf, rg2, ft, fin,
-    loads, hsend, hrecv, send, recv,
+    dg_s, dg, gs, gr, g1, rg1, g2, rg2, ft, fin, h1, rh1, h2, rh2, fs, fins,
+    loads, hsend, hrecv, send, recv, h1send,
 ):
     region, chan = lax.axis_index("region"), lax.axis_index("chan")
     core, z, x = lax.rem(region, 2), lax.rem(lax.div(region, 2), NZ), lax.div(region, 2 * NZ)
@@ -52,9 +52,21 @@
         there = (lax.div(there, 2) * NZ + z) * 2 + lax.rem(there, 2)
         return other, (there, lax.rem(other, NCHAN))
 
-    def xc_peer(step):
-        other = lax.rem(xc + step, NXC)
-        return other, ((lax.div(other, 2) * NZ + z) * 2 + lax.rem(other, 2), chan)
+    parity, z_pair = lax.rem(z, 2), lax.div(z, 2)
+    duo = xc * 2 + parity
+    holder = duo == x * 4
+
+    def duo_device(other):
+        there = lax.div(other, 4) * NZ + z_pair * 2 + lax.rem(other, 2)
+        return there * 2 + lax.rem(lax.div(other, 2), 2), chan
+
+    def duo_peer(step):
+        other = lax.rem(duo + step, NDUO)
+        return other, duo_device(other)
+
+    def line_peer(step):
+        other = lax.rem(z_pair + step, NZ // 2)
+        return other, ((x * NZ + other * 2 + parity) * 2 + core, chan)
 
     def chan_peer(step):
         other = lax.rem(chan + step, NCHAN)
@@ -75,6 +87,7 @@
     greet(z_peer, NZ)
     for device in (lower, upper):
         pl.semaphore_signal(barrier, inc=1, device_id=device, device_id_type=MESH)
+    greet(duo_peer, NDUO)
     greet(plane_peer, NPLANE)
 
     pairs = (
@@ -150,9 +163,6 @@
     basis[0:GROUP] = sky[...]
     pair = rim(0, v0)
 
-    pl.semaphore_wait(barrier, 2 + (NPLANE - 1) + (NZ - 1))
-    halo_start(0)
-
     loaded(cnt, cot)
     counts = cnt[...].astype(F32)
     own_start = jnp.sum(
@@ -167,8 +177,10 @@
         first = (start + off - region) >> 7
         return count, off, first
 
-    def exchange1(k, key, message):
+    def exchange1(k, message):
         s1[k] = message.reshape(NZ, NX, 128)
+
+    def exchange1_start(k, key):
         spread(key, z_peer, NZ, lambda slot: s1.at[k, slot], r1.at[k, z])
         r1[k, z] = s1[k, z]
 
@@ -207,18 +219,7 @@
     lane64 = iota((NZ * NX, NREGION), 1)
     room = jnp.where(lane64 < 64, count0 - off0, count1 - off1)
     message = jnp.where(((lane64 & 63) >> 4) * NREGION < room, message, 0.0)
-    exchange1(0, A1, message)
-    loaded(w1, w2)
-    spread(W1, chan_peer, NCHAN, lambda slot: w1, wg1.at[chan])
-    spread(W2, chan_peer, NCHAN, lambda slot: w2, wg2.at[chan])
-
-    from_row, to_lane = iota((128, 1024), 0), iota((128, 1024), 1)
-    emat[...] = jnp.where(
-        ((from_row >> 4) == (to_lane >> 7))
-        & ((to_lane & 127) == chan * OUT_PART + (from_row & 15)),
-        1.0, 0.0,
-    ).astype(BF16)
-
+    exchange1(0, message)
     gone = jnp.where(region == 0, 0, -1)
     gone_up = jnp.where(region == NREGION - 1, 0, -1)
     links = jnp.where((links >= PIX) & (links < PIX + WW) & (gone == 0), PIX + 2 * WW, links)
@@ -236,7 +237,32 @@
 
     lax.fori_loop(0, (PIX + 2 * WW) // 32, build, 0)
 
-    v1 = finish(0, inner(pair))
+    pl.semaphore_wait(barrier, 2 + (NPLANE - 1) + (NZ - 1) + (NDUO - 1))
+    halo_start(0)
+
+    exchange1_start(0, A1)
+    loaded(w1, w2)
+    spread(W1, chan_peer, NCHAN, lambda slot: w1, wg1.at[chan])
+    spread(W2, chan_peer, NCHAN, lambda slot: w2, wg2.at[chan])
+
+    local = inner(pair)
+    from_row, to_lane = iota((128, 1024), 0), iota((128, 1024), 1)
+    emat[...] = jnp.where(
+        ((from_row >> 4) == (to_lane >> 7))
+        & ((to_lane & 127) == chan * OUT_PART + (from_row & 15)),
+        1.0, 0.0,
+    ).astype(BF16)
+    lane, row = iota((NREGION, NREGION), 1), iota((NREGION, NREGION), 0)
+    xcmajor = (((row >> 5) * NZ + (row & 15)) * 2) + ((row >> 4) & 1)
+    to_pixels = jnp.where(((xcmajor - own_start) & 127) == lane, 1.0, 0.0).astype(BF16)
+    to_rows = jnp.concatenate(
+        [((zmajor + i - own_start) & 127) == lane64 for i in range(2)], axis=1
+    )
+    to_rows = jnp.where(to_rows, 1.0, 0.0).astype(BF16)
+    loaded(cheb)
+    weight = cheb[...]
+    weight_t = weight.astype(F32).T.astype(BF16)
+    v1 = finish(0, local)
     basis[GROUP : 2 * GROUP] = v1.astype(BF16)
     pair = rim(1, v1)
     halo_start(1)
@@ -247,12 +273,6 @@
     halo_start(2)
     local = inner(pair)
     exchange2(0, A1, A2)
-    lane, row = iota((NREGION, NREGION), 1), iota((NREGION, NREGION), 0)
-    xcmajor = (((row >> 5) * NZ + (row & 15)) * 2) + ((row >> 4) & 1)
-    to_pixels = jnp.where(((xcmajor - own_start) & 127) == lane, 1.0, 0.0).astype(BF16)
-    loaded(cheb)
-    weight = cheb[...]
-    weight_t = weight.astype(F32).T.astype(BF16)
     v3 = 2.0 * finish(2, local) - v1
     basis[3 * GROUP :] = v3.astype(BF16)
 
@@ -302,10 +322,8 @@
     outs = jnp.concatenate(
         [jnp.concatenate([outs, empty], axis=1), jnp.concatenate([empty, outs], axis=1)], axis=0
     )
-    to_rows = jnp.concatenate(
-        [((zmajor + i - own_start) & 127) == lane64 for i in range(2)], axis=1
-    )
-    exchange1(1, B1, dot(jnp.where(to_rows, 1.0, 0.0).astype(BF16), outs, 1, 1))
+    exchange1(1, dot(to_rows, outs, 1, 1))
+    exchange1_start(1, B1)
 
     await_bytes(dg.at[pl.ds(0, NCHAN - 1)], recv.at[DG])
     d_conv_t = dg[...].reshape(PIX, 128)
@@ -317,13 +335,29 @@
     grads = gr[0].astype(F32)
     for s in range(1, NCHAN):
         grads = grads + gr[s].astype(F32)
-    g1[:, 0:16] = cheb_part.astype(BF16).reshape(NXC, 16, 128)
-    g1[:, 16:32] = grads[0:128].astype(BF16).reshape(NXC, 16, 128)
+    for i in range(NXC):
+        g1[2 * i] = cheb_part[TILE * i : TILE * (i + 1)].astype(BF16)
+        g1[2 * i + 1] = grads[TILE * i : TILE * (i + 1)].astype(BF16)
     for i in range(NX):
-        g1[2 * i, 32:48] = grads[128 + 16 * i : 144 + 16 * i].astype(BF16)
-        g1[2 * i + 1, 32:48] = jnp.zeros((16, 128), BF16)
-    spread(G1, xc_peer, NXC, lambda slot: g1.at[slot], rg1.at[xc])
-    rg1[xc] = g1[xc]
+        h1[i] = grads[128 + TILE * i : 128 + TILE * (i + 1)].astype(BF16)
+    spread(G1, duo_peer, NDUO, lambda slot: g1.at[slot], rg1.at[duo])
+
+    def to_holder(i):
+        return pltpu.make_async_remote_copy(
+            src_ref=h1.at[i], dst_ref=rh1.at[duo], send_sem=h1send.at[i], recv_sem=recv.at[H1],
+            device_id=duo_device(4 * i), device_id_type=MESH,
+        )
+
+    for i in range(NX):
+        @pl.when(duo != 4 * i)
+        def _(i=i):
+            to_holder(i).start()
+
+        @pl.when(duo == 4 * i)
+        def _(i=i):
+            rh1[duo] = h1[i]
+
+    rg1[duo] = g1[duo]
     local = inner(pair)
     d_low = dot(weight[: 3 * GROUP], d_conv_t, 1, 1)
     adj2 = d_low[2 * GROUP :] + 2.0 * finish(3, local)
@@ -331,17 +365,24 @@
     pair = rim(4, adj2)
     halo_start(4)
 
-    await_bytes(rg1.at[pl.ds(0, NXC - 1)], recv.at[G1])
-    total = rg1[0].astype(F32)
-    for s in range(1, NXC):
-        total = total + rg1[s].astype(F32)
-    hbuf[...] = total.astype(BF16)
-    for own_core, rows in ((0, PIECE), (1, CORE1)):
-        @pl.when(core == own_core)
-        def _(rows=rows):
-            spread(G2, z_peer, NZ, lambda slot: hbuf.at[pl.ds(0, rows)], rg2.at[z, pl.ds(0, rows)])
-
-    rg2[z] = hbuf[...]
+    def sum_of(ref, count):
+        total = ref[0].astype(F32)
+        for s in range(1, count):
+            total = total + ref[s].astype(F32)
+        return total.astype(BF16)
+
+    await_bytes(rg1.at[pl.ds(0, NDUO - 1)], recv.at[G1])
+    g2[...] = sum_of(rg1, NDUO)
+    spread(G2, line_peer, NZ // 2, lambda slot: g2, rg2.at[z_pair])
+    rg2[z_pair] = g2[...]
+
+    @pl.when(holder)
+    def _():
+        await_bytes(rh1.at[pl.ds(0, NDUO - 1)], recv.at[H1])
+        h2[...] = sum_of(rh1, NDUO)
+        spread(H2, line_peer, NZ // 2, lambda slot: h2, rh2.at[z_pair])
+        rh2[z_pair] = h2[...]
+
     exchange2(1, B1, B2)
     local = inner(pair)
     count2, off2, first2 = places(xcmajor)
@@ -357,32 +398,35 @@
     local = inner(pair)
     ig_out[...] = adj0 + finish(5, local)
 
-    for own_core, rows in ((0, PIECE), (1, CORE1)):
-        @pl.when(core == own_core)
-        def _(rows=rows):
-            await_bytes(rg2.at[pl.ds(0, NZ - 1), pl.ds(0, rows)], recv.at[G2])
-            total = rg2[0, 0:rows].astype(F32)
-            for s in range(1, NZ):
-                total = total + rg2[s, 0:rows].astype(F32)
-            ft[0:rows] = total.astype(BF16)
-            if rows < PIECE:
-                ft[rows:] = jnp.zeros((PIECE - rows, 128), BF16)
-
-    spread(F2, xc_peer, NXC, lambda slot: ft, fin.at[xc])
-    fin[xc] = ft[...]
-
     rows_t = arrived2(1, B2)
     result = jnp.zeros((OUT_PART, ROWS_DEV), F32)
     for s in range(4):
         result = result + dot(rows_t[s * OUT_PART : (s + 1) * OUT_PART], mmat[s])
     mo_out[...] = result.astype(BF16)
 
+    await_bytes(rg2.at[pl.ds(0, NZ // 2 - 1)], recv.at[G2])
+    ft[...] = sum_of(rg2, NZ // 2)
+    spread(F2, duo_peer, NDUO, lambda slot: ft, fin.at[duo])
+    fin[duo] = ft[...]
+
+    @pl.when(holder)
+    def _():
+        await_bytes(rh2.at[pl.ds(0, NZ // 2 - 1)], recv.at[H2])
+        fs[...] = sum_of(rh2, NZ // 2)
+        spread(I2, duo_peer, NDUO, lambda slot: fs, fins.at[x])
+        fins[x] = fs[...]
+        await_bytes(fins.at[pl.ds(0, NX - 1)], recv.at[I2])
+
+    @pl.when(jnp.logical_not(holder))
+    def _():
+        await_bytes(fins, recv.at[I2])
+
     scale = 1.0 / math.sqrt(NREGION * ROWS_DEV)
-    await_bytes(fin.at[pl.ds(0, NXC - 1)], recv.at[F2])
-    cg_out[...] = fin[:, 0:16].astype(F32).reshape(128, 128) * scale
-    fg_out[...] = fin[:, 16:32].astype(F32).reshape(128, 128) * scale
-    for i in range(NX):
-        sg_out[16 * i : 16 * (i + 1)] = fin[2 * i, 32:48].astype(F32) * scale
+    await_bytes(fin.at[pl.ds(0, NDUO - 1)], recv.at[F2])
+    for i in range(NXC):
+        cg_out[TILE * i : TILE * (i + 1)] = fin[2 * i].astype(F32) * scale
+        fg_out[TILE * i : TILE * (i + 1)] = fin[2 * i + 1].astype(F32) * scale
+    sg_out[...] = fins[...].astype(F32).reshape(OUTF, 128) * scale
 
     for step in range(6):
         for side in range(2):
@@ -392,22 +436,24 @@
     for k, key1, key2 in ((0, A1, A2), (1, B1, B2)):
         await_bytes(r1.at[k, pl.ds(0, NZ - 1)], send.at[key1])
         await_bytes(r2.at[k, pl.ds(0, NPLANE - 1)], send.at[key2])
-    await_bytes(rg1.at[pl.ds(0, NXC - 1)], send.at[G1])
-    await_bytes(fin.at[pl.ds(0, NXC - 1)], send.at[F2])
-    for own_core, rows in ((0, PIECE), (1, CORE1)):
-        @pl.when(core == own_core)
-        def _(rows=rows):
-            await_bytes(rg2.at[pl.ds(0, NZ - 1), pl.ds(0, rows)], send.at[G2])
+    await_bytes(rg1.at[pl.ds(0, NDUO - 1)], send.at[G1])
+    await_bytes(rg2.at[pl.ds(0, NZ // 2 - 1)], send.at[G2])
+    await_bytes(fin.at[pl.ds(0, NDUO - 1)], send.at[F2])
+    for i in range(NX):
+        @pl.when(duo != 4 * i)
+        def _(i=i):
+            to_holder(i).wait_send()
+
+    @pl.when(holder)
+    def _():
+        await_bytes(rh2.at[pl.ds(0, NZ // 2 - 1)], send.at[H2])
+        await_bytes(rh1.at[pl.ds(0, NDUO - 1)], send.at[I2])
 
 
 def writer(*refs):
     count = len(refs) // 2
-    sems = refs[-1]
-    copies = [pltpu.make_async_copy(refs[i], refs[count + i], sems.at[i]) for i in range(count)]
-    for copy in copies:
-        copy.start()
-    for copy in copies:
-        copy.wait()
+    for i in range(count):
+        refs[count + i][...] = refs[i][...]
 
 
 def body(
@@ -447,17 +493,24 @@
         vmem((NCHAN, WW, 128), BF16),
         vmem((NCHAN, 192, 128), BF16),
         vmem((NCHAN, 192, 128), BF16),
-        vmem((NXC, PIECE, 128), BF16),
-        vmem((NXC, PIECE, 128), BF16),
-        vmem((PIECE, 128), BF16),
-        vmem((NZ, PIECE, 128), BF16),
-        vmem((PIECE, 128), BF16),
-        vmem((NXC, PIECE, 128), BF16),
+        vmem((NDUO, TILE, 128), BF16),
+        vmem((NDUO, TILE, 128), BF16),
+        vmem((TILE, 128), BF16),
+        vmem((NZ // 2, TILE, 128), BF16),
+        vmem((TILE, 128), BF16),
+        vmem((NDUO, TILE, 128), BF16),
+        vmem((NX, TILE, 128), BF16),
+        vmem((NDUO, TILE, 128), BF16),
+        vmem((TILE, 128), BF16),
+        vmem((NZ // 2, TILE, 128), BF16),
+        vmem((TILE, 128), BF16),
+        vmem((NX, TILE, 128), BF16),
         dma((8,)),
         dma((6, 2)),
         dma((6, 2)),
         dma((EXCHANGES,)),
         dma((EXCHANGES,)),
+        dma((NX,)),
     ]
     results = (
         shape((OUT_PART, ROWS_DEV), BF16),
@@ -482,9 +535,9 @@
     mlp_out, input_grad, cheb_grad, first_grad, second_grad = pl.pallas_call(
         writer,
         out_shape=results,
-        in_specs=[pl.BlockSpec(memory_space=pl.ANY)] * 5,
-        out_specs=[pl.BlockSpec(memory_space=pl.ANY)] * 5,
-        scratch_shapes=[dma((5,))],
+        in_specs=[pl.BlockSpec(memory_space=vmem)] * 5,
+        out_specs=[pl.BlockSpec(memory_space=vmem)] * 5,
+        compiler_params=pltpu.CompilerParams(vmem_limit_bytes=60 * 1024 * 1024),
     )(*found)
     return mlp_out, input_grad, cheb_grad.reshape(ORDER, GROUP, 128), first_grad, second_grad.T
 

time: 69.7 us -> 57 us (0.82)
  Pallas kernels: 68.8 us -> 56.2 us
    pallas_call x1, Pallas kernels: 8.35 us -> 1.61 us  [body(): pl.pallas_call(writer, out_shape=results, in_specs=[pl.BlockSpec(memory_s...]
    pallas_call x1, Pallas kernels: 60.5 us -> 54.5 us  [body(): pl.pallas_call(kernel, out_shape=results, in_specs=[pl.BlockSpec(memory_s...]
where the time goes in v3:
time: 57 us; the launch traced here: 56.8 us
  Pallas kernels  56.2 us (99%)
  between operations  0.64 us (1%)
    pallas_call x1, Pallas kernels, body(): pl.pallas_call(kernel, out_shape=results, in_specs=[pl.BlockSpec(memory_s...  54.5 us
    pallas_call x1, Pallas kernels, body(): pl.pallas_call(writer, out_shape=results, in_specs=[pl.BlockSpec(memory_s...  1.61 us

profile of v3, /device:TPU:1, one launch (start us, length us, event | category | flops | bytes accessed | tf_op | source)
XLA Modules:
  0.0 56.8 jit_solution(5962534713937663474)
XLA Ops:
  0.6 54.5 %shard_map.119 = (bf16[16,256]{1,0:T(8,128)(2,1)}, f32[32,512]{1,0:T(8,128)}, f32[128,128]{1,0:T(8,128)}, f32[128,128]{1,0:T(8,128)}, f32[64,128]{1,0:T(8,128)}) custom-call(bf16[32,512]{1,0:T(8,128)(2,1)} %sky_in.1, s32[8,512]{1,0:T(8,128)} %nb_in.1, s32[2,128]{1,0:T(2,128)} %sl_in.1, s32[1,128]{1,0:T(1,128)} %bitcast.9, bf16[128,128]{1,0:T(8,128)(2,1)} %bitcast.6, ...), custom_call_target="tpu_custom_call" | custom-call | flops 600000000 | bytes 1000000 | tf_op jit(solution)/shard_map/pallas_call | solution.py:522
  55.2 1.6 %shard_map.120 = (bf16[16,256]{1,0:T(8,128)(2,1)}, f32[32,512]{1,0:T(8,128)}, f32[128,128]{1,0:T(8,128)}, f32[128,128]{1,0:T(8,128)}, f32[64,128]{1,0:T(8,128)}) custom-call(bf16[16,256]{1,0:T(8,128)(2,1)} %get-tuple-element.15.refs_0_, f32[32,512]{1,0:T(8,128)} %get-tuple-element.16.refs_1_, f32[128,128]{1,0:T(8,128)} %get-tuple-element.17.refs_2_, ...), custom_call_target="tpu_custom_call" | custom-call | tf_op jit(solution)/shard_map/pallas_call | solution.py:535

commit v4 on v3

--- a/solution.py
+++ b/solution.py
@@ -15,7 +15,8 @@
 NDUO, TILE = 16, 16
 OUT_PART, ROWS_DEV, OUTF = 16, 256, 64
 
-W1, W2, A1, A2, CP, DG, GS, B1, B2, G1, G2, F2, H1, H2, I2, EXCHANGES = range(16)
+W1, W2, W3, A1, A2, C0, DG, GS, B1, B2, G1, G2, F2, H1, H2, I2 = [*range(6), *range(9, 19)]
+EXCHANGES = 19
 
 
 def dot(left, right, left_dim=1, right_dim=0):
@@ -32,7 +33,7 @@
     sky_in, nb_in, sl_in, cnt_in, cheb_in, w1_in, w2_in, cot_in,
     mo_out, ig_out, cg_out, fg_out, sg_out,
     sky, nb, sl, cnt, cheb, w1, w2, cot,
-    amat, smat, mmat, emat, basis, hs, hr, wg1, wg2, s1, r1, s2, r2, cp, cr, dhid,
+    amat, smat, mmat, emat, basis, hs, hr, wg1, wg2, s1, r1, s2, r2, wt, wgt, bs, bq,
     dg_s, dg, gs, gr, g1, rg1, g2, rg2, ft, fin, h1, rh1, h2, rh2, fs, fins,
     loads, hsend, hrecv, send, recv, h1send,
 ):
@@ -159,8 +160,17 @@
         local = local + dot(hr[step, 1], amat[PIX + WW :])
         return -inv * local
 
+    def keep(level, values):
+        basis[level * GROUP : (level + 1) * GROUP] = values
+        for s in range(NCHAN):
+            bs[level, s] = values[:, s * WW : (s + 1) * WW]
+
+    def share(level):
+        spread(C0 + level, chan_peer, NCHAN, lambda slot: bs.at[level, slot], bq.at[chan, level])
+        bq[chan, level] = bs[level, chan]
+
     v0 = sky[...].astype(F32)
-    basis[0:GROUP] = sky[...]
+    keep(0, sky[...])
     pair = rim(0, v0)
 
     loaded(cnt, cot)
@@ -238,13 +248,21 @@
     lax.fori_loop(0, (PIX + 2 * WW) // 32, build, 0)
 
     pl.semaphore_wait(barrier, 2 + (NPLANE - 1) + (NZ - 1) + (NDUO - 1))
+    exchange1_start(0, A1)
     halo_start(0)
-
-    exchange1_start(0, A1)
     loaded(w1, w2)
     spread(W1, chan_peer, NCHAN, lambda slot: w1, wg1.at[chan])
     spread(W2, chan_peer, NCHAN, lambda slot: w2, wg2.at[chan])
 
+    loaded(cheb)
+    weight = cheb[...]
+    wt[...] = weight.astype(F32).T.astype(BF16)
+    spread(W3, chan_peer, NCHAN, lambda slot: wt, wgt.at[chan])
+    wg1[chan] = w1[...]
+    wg2[chan] = w2[...]
+    wgt[chan] = wt[...]
+
+    share(0)
     local = inner(pair)
     from_row, to_lane = iota((128, 1024), 0), iota((128, 1024), 1)
     emat[...] = jnp.where(
@@ -259,58 +277,53 @@
         [((zmajor + i - own_start) & 127) == lane64 for i in range(2)], axis=1
     )
     to_rows = jnp.where(to_rows, 1.0, 0.0).astype(BF16)
-    loaded(cheb)
-    weight = cheb[...]
-    weight_t = weight.astype(F32).T.astype(BF16)
     v1 = finish(0, local)
-    basis[GROUP : 2 * GROUP] = v1.astype(BF16)
     pair = rim(1, v1)
     halo_start(1)
+    keep(1, v1.astype(BF16))
+    share(1)
     local = inner(pair)
     v2 = 2.0 * finish(1, local) - v0
-    basis[2 * GROUP : 3 * GROUP] = v2.astype(BF16)
     pair = rim(2, v2)
     halo_start(2)
+    keep(2, v2.astype(BF16))
+    share(2)
     local = inner(pair)
     exchange2(0, A1, A2)
     v3 = 2.0 * finish(2, local) - v1
-    basis[3 * GROUP :] = v3.astype(BF16)
-
-    part = dot(weight_t, basis[...]).astype(BF16)
-    for s in range(NCHAN):
-        cp[s] = part[:, s * WW : (s + 1) * WW]
-    spread(CP, chan_peer, NCHAN, lambda slot: cp.at[slot], cr.at[chan])
-    cr[chan] = cp[chan]
-
-    wg1[chan] = w1[...]
-    wg2[chan] = w2[...]
+    keep(3, v3.astype(BF16))
+    share(3)
+
     await_bytes(wg2.at[pl.ds(0, NCHAN - 1)], recv.at[W2])
     await_bytes(wg1.at[pl.ds(0, NCHAN - 1)], recv.at[W1])
-    columns = dot(arrived2(0, A2), to_pixels)[:OUTF]
-    cot_px = columns.astype(BF16)
-    cot_t = columns.T.astype(BF16)
-    for h in range(NCHAN):
-        dhid[h] = dot(cot_t, wg2[h])
-
-    await_bytes(cr.at[pl.ds(0, NCHAN - 1)], recv.at[CP])
-    total = cr[0].astype(F32)
-    for s in range(1, NCHAN):
-        total = total + cr[s].astype(F32)
-    features = total.astype(BF16)
-    features_t = total.T.astype(BF16)
-    hidden, d_pre = [], []
-    d_feat = jnp.zeros((WW, 128), F32)
+    await_bytes(wgt.at[pl.ds(0, NCHAN - 1)], recv.at[W3])
+    for level in range(ORDER):
+        await_bytes(bq.at[pl.ds(0, NCHAN - 1), level], recv.at[C0 + level])
+    conv = jnp.zeros((128, WW), F32)
+    for s in range(NCHAN):
+        conv = conv + dot(wgt[s], bq[s].reshape(ORDER * GROUP, WW))
+    features = conv.astype(BF16)
+    features_t = conv.T.astype(BF16)
+    hidden, slope = [], []
+    out_t = jnp.zeros((WW, OUTF), F32)
     for h in range(NCHAN):
         pre = dot(features_t, wg1[h])
         gate = jax.nn.sigmoid(pre)
         hidden.append((pre * gate).astype(BF16))
-        d_pre.append((dhid[h] * gate * (1.0 + pre * (1.0 - gate))).astype(BF16))
+        slope.append(gate * (1.0 + pre * (1.0 - gate)))
+
+    columns = dot(arrived2(0, A2), to_pixels)[:OUTF]
+    cot_px = columns.astype(BF16)
+    cot_t = columns.T.astype(BF16)
+    d_pre = []
+    d_feat = jnp.zeros((WW, 128), F32)
+    for h in range(NCHAN):
+        d_pre.append((dot(cot_t, wg2[h]) * slope[h]).astype(BF16))
         d_feat = d_feat + dot(d_pre[h], wg1[h], 1, 1)
     dg_s[...] = d_feat.astype(BF16)
     spread(DG, chan_peer, NCHAN, lambda slot: dg_s, dg.at[chan])
     dg[chan] = dg_s[...]
 
-    out_t = jnp.zeros((WW, OUTF), F32)
     for h in range(NCHAN):
         gs[h, 0:128] = dot(features, d_pre[h]).astype(BF16)
         gs[h, 128:192] = dot(cot_px, hidden[h]).astype(BF16)
@@ -327,20 +340,38 @@
 
     await_bytes(dg.at[pl.ds(0, NCHAN - 1)], recv.at[DG])
     d_conv_t = dg[...].reshape(PIX, 128)
+    cheb_part = dot(basis[...], d_conv_t)
+    for i in range(NXC):
+        g1[2 * i] = cheb_part[TILE * i : TILE * (i + 1)].astype(BF16)
+
+    def to_half(half):
+        def step(d, carry):
+            other = 2 * d + half
+
+            @pl.when(other != duo)
+            def _():
+                pltpu.make_async_remote_copy(
+                    src_ref=g1.at[other], dst_ref=rg1.at[duo], send_sem=send.at[G1],
+                    recv_sem=recv.at[G1], device_id=duo_device(other), device_id_type=MESH,
+                ).start()
+
+            return carry
+
+        lax.fori_loop(0, NDUO // 2, step, 0)
+
+    to_half(0)
     adj3 = dot(weight[3 * GROUP :], d_conv_t, 1, 1)
     pair = rim(3, adj3)
     halo_start(3)
-    cheb_part = dot(basis[...], d_conv_t)
     await_bytes(gr.at[pl.ds(0, NCHAN - 1)], recv.at[GS])
     grads = gr[0].astype(F32)
     for s in range(1, NCHAN):
         grads = grads + gr[s].astype(F32)
     for i in range(NXC):
-        g1[2 * i] = cheb_part[TILE * i : TILE * (i + 1)].astype(BF16)
         g1[2 * i + 1] = grads[TILE * i : TILE * (i + 1)].astype(BF16)
+    to_half(1)
     for i in range(NX):
         h1[i] = grads[128 + TILE * i : 128 + TILE * (i + 1)].astype(BF16)
-    spread(G1, duo_peer, NDUO, lambda slot: g1.at[slot], rg1.at[duo])
 
     def to_holder(i):
         return pltpu.make_async_remote_copy(
@@ -431,8 +462,10 @@
     for step in range(6):
         for side in range(2):
             halo_copy(step, side).wait_send()
-    for key, ref in ((W1, wg1), (W2, wg2), (CP, cr), (DG, dg), (GS, gr)):
+    for key, ref in ((W1, wg1), (W2, wg2), (W3, wgt), (DG, dg), (GS, gr)):
         await_bytes(ref.at[pl.ds(0, NCHAN - 1)], send.at[key])
+    for level in range(ORDER):
+        await_bytes(bq.at[pl.ds(0, NCHAN - 1), level], send.at[C0 + level])
     for k, key1, key2 in ((0, A1, A2), (1, B1, B2)):
         await_bytes(r1.at[k, pl.ds(0, NZ - 1)], send.at[key1])
         await_bytes(r2.at[k, pl.ds(0, NPLANE - 1)], send.at[key2])
@@ -486,9 +519,10 @@
         vmem((2, NZ, NX, 128), F32),
         vmem((2, NPLANE, NZ, 128), BF16),
         vmem((2, NPLANE, NZ, 128), BF16),
-        vmem((NCHAN, 128, WW), BF16),
-        vmem((NCHAN, 128, WW), BF16),
-        vmem((NCHAN, WW, 128), F32),
+        vmem((128, ORDER * GROUP), BF16),
+        vmem((NCHAN, 128, ORDER * GROUP), BF16),
+        vmem((ORDER, NCHAN, GROUP, WW), BF16),
+        vmem((NCHAN, ORDER, GROUP, WW), BF16),
         vmem((WW, 128), BF16),
         vmem((NCHAN, WW, 128), BF16),
         vmem((NCHAN, 192, 128), BF16),

time: 57 us -> 56.7 us (level)
  no operation moved by 1% of the time
where the time goes in v4:
time: 56.7 us; the launch traced here: 56.5 us
  Pallas kernels  55.9 us (99%)
  between operations  0.64 us (1%)
    pallas_call x1, Pallas kernels, body(): pl.pallas_call(kernel, out_shape=results, in_specs=[pl.BlockSpec(memory_s...  54.3 us
    pallas_call x1, Pallas kernels, body(): pl.pallas_call(writer, out_shape=results, in_specs=[pl.BlockSpec(memory_s...  1.61 us

profile of v4, /device:TPU:1, one launch (start us, length us, event | category | flops | bytes accessed | tf_op | source)
XLA Modules:
  0.0 56.5 jit_solution(10574181229518897591)
XLA Ops:
  0.6 54.3 %shard_map.119 = (bf16[16,256]{1,0:T(8,128)(2,1)}, f32[32,512]{1,0:T(8,128)}, f32[128,128]{1,0:T(8,128)}, f32[128,128]{1,0:T(8,128)}, f32[64,128]{1,0:T(8,128)}) custom-call(bf16[32,512]{1,0:T(8,128)(2,1)} %sky_in.1, s32[8,512]{1,0:T(8,128)} %nb_in.1, s32[2,128]{1,0:T(2,128)} %sl_in.1, s32[1,128]{1,0:T(1,128)} %bitcast.9, bf16[128,128]{1,0:T(8,128)(2,1)} %bitcast.6, ...), custom_call_target="tpu_custom_call" | custom-call | flops 600000000 | bytes 1000000 | tf_op jit(solution)/shard_map/pallas_call | solution.py:556
  54.9 1.6 %shard_map.120 = (bf16[16,256]{1,0:T(8,128)(2,1)}, f32[32,512]{1,0:T(8,128)}, f32[128,128]{1,0:T(8,128)}, f32[128,128]{1,0:T(8,128)}, f32[64,128]{1,0:T(8,128)}) custom-call(bf16[16,256]{1,0:T(8,128)(2,1)} %get-tuple-element.15.refs_0_, f32[32,512]{1,0:T(8,128)} %get-tuple-element.16.refs_1_, f32[128,128]{1,0:T(8,128)} %get-tuple-element.17.refs_2_, ...), custom_call_target="tpu_custom_call" | custom-call | tf_op jit(solution)/shard_map/pallas_call | solution.py:569

commit v5 on v4

--- a/solution.py
+++ b/solution.py
@@ -12,7 +12,7 @@
 PIX, WW, ORDER, GROUP = 512, 128, 4, 32
 NZ, NX, NXC, NCHAN, NREGION = 16, 4, 8, 4, 128
 NPLANE = NXC * NCHAN
-NDUO, TILE = 16, 16
+NDUO, NQUAD, TILE = 16, 64, 16
 OUT_PART, ROWS_DEV, OUTF = 16, 256, 64
 
 W1, W2, W3, A1, A2, C0, DG, GS, B1, B2, G1, G2, F2, H1, H2, I2 = [*range(6), *range(9, 19)]
@@ -35,7 +35,7 @@
     sky, nb, sl, cnt, cheb, w1, w2, cot,
     amat, smat, mmat, emat, basis, hs, hr, wg1, wg2, s1, r1, s2, r2, wt, wgt, bs, bq,
     dg_s, dg, gs, gr, g1, rg1, g2, rg2, ft, fin, h1, rh1, h2, rh2, fs, fins,
-    loads, hsend, hrecv, send, recv, h1send,
+    loads, hsend, hrecv, send, recv,
 ):
     region, chan = lax.axis_index("region"), lax.axis_index("chan")
     core, z, x = lax.rem(region, 2), lax.rem(lax.div(region, 2), NZ), lax.div(region, 2 * NZ)
@@ -65,6 +65,15 @@
         other = lax.rem(duo + step, NDUO)
         return other, duo_device(other)
 
+    quad = duo * NCHAN + chan
+
+    def quad_device(there, other_chan):
+        return duo_device(there)[0], other_chan
+
+    def quad_peer(step):
+        other = lax.rem(quad + step, NQUAD)
+        return other, quad_device(lax.div(other, NCHAN), lax.rem(other, NCHAN))
+
     def line_peer(step):
         other = lax.rem(z_pair + step, NZ // 2)
         return other, ((x * NZ + other * 2 + parity) * 2 + core, chan)
@@ -88,8 +97,7 @@
     greet(z_peer, NZ)
     for device in (lower, upper):
         pl.semaphore_signal(barrier, inc=1, device_id=device, device_id_type=MESH)
-    greet(duo_peer, NDUO)
-    greet(plane_peer, NPLANE)
+    greet(quad_peer, NQUAD)
 
     pairs = (
         (nb_in, nb), (sl_in, sl), (sky_in, sky), (cnt_in, cnt),
@@ -247,7 +255,7 @@
 
     lax.fori_loop(0, (PIX + 2 * WW) // 32, build, 0)
 
-    pl.semaphore_wait(barrier, 2 + (NPLANE - 1) + (NZ - 1) + (NDUO - 1))
+    pl.semaphore_wait(barrier, 2 + (NQUAD - 1) + (NZ - 1))
     exchange1_start(0, A1)
     halo_start(0)
     loaded(w1, w2)
@@ -325,11 +333,42 @@
     dg[chan] = dg_s[...]
 
     for h in range(NCHAN):
-        gs[h, 0:128] = dot(features, d_pre[h]).astype(BF16)
-        gs[h, 128:192] = dot(cot_px, hidden[h]).astype(BF16)
+        first = dot(features, d_pre[h]).astype(BF16)
+        second = dot(cot_px, hidden[h]).astype(BF16)
         out_t = out_t + dot(hidden[h], wg2[h], 1, 1)
-    spread(GS, chan_peer, NCHAN, lambda slot: gs.at[slot], gr.at[chan])
-    gr[chan] = gs[chan]
+        for i in range(NXC):
+            gs[i * NCHAN + h] = first[TILE * i : TILE * (i + 1)]
+        for i in range(NX):
+            h1[i * NCHAN + h] = second[TILE * i : TILE * (i + 1)]
+
+    def scatter(key, count, mine, duo_of, src, dst):
+        def step(d, carry):
+            slot = lax.rem(mine + d, count)
+            there, other_chan = duo_of(lax.div(slot, NCHAN)), lax.rem(slot, NCHAN)
+
+            @pl.when(there * NCHAN + other_chan != quad)
+            def _():
+                pltpu.make_async_remote_copy(
+                    src_ref=src.at[slot], dst_ref=dst.at[quad], send_sem=send.at[key],
+                    recv_sem=recv.at[key], device_id=quad_device(there, other_chan),
+                    device_id_type=MESH,
+                ).start()
+
+            return carry
+
+        lax.fori_loop(0, count, step, 0)
+
+    scatter(GS, NPLANE, plane, lambda i: 2 * i + 1, gs, gr)
+    scatter(H1, NX * NCHAN, x * NCHAN + chan, lambda i: 4 * i, h1, rh1)
+
+    @pl.when(parity == 1)
+    def _():
+        gr[quad] = gs[plane]
+
+    @pl.when(holder)
+    def _():
+        rh1[quad] = h1[x * NCHAN + chan]
+
     outs = out_t.T.astype(BF16)
     empty = jnp.zeros_like(outs)
     outs = jnp.concatenate(
@@ -342,53 +381,29 @@
     d_conv_t = dg[...].reshape(PIX, 128)
     cheb_part = dot(basis[...], d_conv_t)
     for i in range(NXC):
-        g1[2 * i] = cheb_part[TILE * i : TILE * (i + 1)].astype(BF16)
-
-    def to_half(half):
-        def step(d, carry):
-            other = 2 * d + half
-
-            @pl.when(other != duo)
-            def _():
-                pltpu.make_async_remote_copy(
-                    src_ref=g1.at[other], dst_ref=rg1.at[duo], send_sem=send.at[G1],
-                    recv_sem=recv.at[G1], device_id=duo_device(other), device_id_type=MESH,
-                ).start()
-
-            return carry
-
-        lax.fori_loop(0, NDUO // 2, step, 0)
-
-    to_half(0)
+        g1[i] = cheb_part[TILE * i : TILE * (i + 1)].astype(BF16)
+
+    def cheb_step(d, carry):
+        slot = lax.rem(xc + d, NXC)
+
+        @pl.when(2 * slot != duo)
+        def _():
+            pltpu.make_async_remote_copy(
+                src_ref=g1.at[slot], dst_ref=rg1.at[duo], send_sem=send.at[G1],
+                recv_sem=recv.at[G1], device_id=duo_device(2 * slot), device_id_type=MESH,
+            ).start()
+
+        return carry
+
+    lax.fori_loop(0, NXC, cheb_step, 0)
+
+    @pl.when(parity == 0)
+    def _():
+        rg1[duo] = g1[xc]
+
     adj3 = dot(weight[3 * GROUP :], d_conv_t, 1, 1)
     pair = rim(3, adj3)
     halo_start(3)
-    await_bytes(gr.at[pl.ds(0, NCHAN - 1)], recv.at[GS])
-    grads = gr[0].astype(F32)
-    for s in range(1, NCHAN):
-        grads = grads + gr[s].astype(F32)
-    for i in range(NXC):
-        g1[2 * i + 1] = grads[TILE * i : TILE * (i + 1)].astype(BF16)
-    to_half(1)
-    for i in range(NX):
-        h1[i] = grads[128 + TILE * i : 128 + TILE * (i + 1)].astype(BF16)
-
-    def to_holder(i):
-        return pltpu.make_async_remote_copy(
-            src_ref=h1.at[i], dst_ref=rh1.at[duo], send_sem=h1send.at[i], recv_sem=recv.at[H1],
-            device_id=duo_device(4 * i), device_id_type=MESH,
-        )
-
-    for i in range(NX):
-        @pl.when(duo != 4 * i)
-        def _(i=i):
-            to_holder(i).start()
-
-        @pl.when(duo == 4 * i)
-        def _(i=i):
-            rh1[duo] = h1[i]
-
-    rg1[duo] = g1[duo]
     local = inner(pair)
     d_low = dot(weight[: 3 * GROUP], d_conv_t, 1, 1)
     adj2 = d_low[2 * GROUP :] + 2.0 * finish(3, local)
@@ -402,15 +417,23 @@
             total = total + ref[s].astype(F32)
         return total.astype(BF16)
 
-    await_bytes(rg1.at[pl.ds(0, NDUO - 1)], recv.at[G1])
-    g2[...] = sum_of(rg1, NDUO)
+    @pl.when(parity == 0)
+    def _():
+        await_bytes(rg1.at[pl.ds(0, NDUO - 1)], recv.at[G1])
+        g2[...] = sum_of(rg1, NDUO)
+
+    @pl.when(parity == 1)
+    def _():
+        await_bytes(gr.at[pl.ds(0, NQUAD - 1)], recv.at[GS])
+        g2[...] = sum_of(gr, NQUAD)
+
     spread(G2, line_peer, NZ // 2, lambda slot: g2, rg2.at[z_pair])
     rg2[z_pair] = g2[...]
 
     @pl.when(holder)
     def _():
-        await_bytes(rh1.at[pl.ds(0, NDUO - 1)], recv.at[H1])
-        h2[...] = sum_of(rh1, NDUO)
+        await_bytes(rh1.at[pl.ds(0, NQUAD - 1)], recv.at[H1])
+        h2[...] = sum_of(rh1, NQUAD)
         spread(H2, line_peer, NZ // 2, lambda slot: h2, rh2.at[z_pair])
         rh2[z_pair] = h2[...]
 
@@ -462,23 +485,28 @@
     for step in range(6):
         for side in range(2):
             halo_copy(step, side).wait_send()
-    for key, ref in ((W1, wg1), (W2, wg2), (W3, wgt), (DG, dg), (GS, gr)):
+    for key, ref in ((W1, wg1), (W2, wg2), (W3, wgt), (DG, dg)):
         await_bytes(ref.at[pl.ds(0, NCHAN - 1)], send.at[key])
     for level in range(ORDER):
         await_bytes(bq.at[pl.ds(0, NCHAN - 1), level], send.at[C0 + level])
     for k, key1, key2 in ((0, A1, A2), (1, B1, B2)):
         await_bytes(r1.at[k, pl.ds(0, NZ - 1)], send.at[key1])
         await_bytes(r2.at[k, pl.ds(0, NPLANE - 1)], send.at[key2])
-    await_bytes(rg1.at[pl.ds(0, NDUO - 1)], send.at[G1])
+    for own_parity in range(2):
+        @pl.when(parity == own_parity)
+        def _(own_parity=own_parity):
+            await_bytes(rg1.at[pl.ds(0, NXC - 1 + own_parity)], send.at[G1])
+            await_bytes(gr.at[pl.ds(0, NPLANE - own_parity)], send.at[GS])
+
     await_bytes(rg2.at[pl.ds(0, NZ // 2 - 1)], send.at[G2])
     await_bytes(fin.at[pl.ds(0, NDUO - 1)], send.at[F2])
-    for i in range(NX):
-        @pl.when(duo != 4 * i)
-        def _(i=i):
-            to_holder(i).wait_send()
+    @pl.when(jnp.logical_not(holder))
+    def _():
+        await_bytes(rh1.at[pl.ds(0, NX * NCHAN)], send.at[H1])
 
     @pl.when(holder)
     def _():
+        await_bytes(rh1.at[pl.ds(0, NX * NCHAN - 1)], send.at[H1])
         await_bytes(rh2.at[pl.ds(0, NZ // 2 - 1)], send.at[H2])
         await_bytes(rh1.at[pl.ds(0, NDUO - 1)], send.at[I2])
 
@@ -525,16 +553,16 @@
         vmem((NCHAN, ORDER, GROUP, WW), BF16),
         vmem((WW, 128), BF16),
         vmem((NCHAN, WW, 128), BF16),
-        vmem((NCHAN, 192, 128), BF16),
-        vmem((NCHAN, 192, 128), BF16),
-        vmem((NDUO, TILE, 128), BF16),
+        vmem((NPLANE, TILE, 128), BF16),
+        vmem((NQUAD, TILE, 128), BF16),
+        vmem((NXC, TILE, 128), BF16),
         vmem((NDUO, TILE, 128), BF16),
         vmem((TILE, 128), BF16),
         vmem((NZ // 2, TILE, 128), BF16),
         vmem((TILE, 128), BF16),
         vmem((NDUO, TILE, 128), BF16),
-        vmem((NX, TILE, 128), BF16),
-        vmem((NDUO, TILE, 128), BF16),
+        vmem((NX * NCHAN, TILE, 128), BF16),
+        vmem((NQUAD, TILE, 128), BF16),
         vmem((TILE, 128), BF16),
         vmem((NZ // 2, TILE, 128), BF16),
         vmem((TILE, 128), BF16),
@@ -544,7 +572,6 @@
         dma((6, 2)),
         dma((EXCHANGES,)),
         dma((EXCHANGES,)),
-        dma((NX,)),
     ]
     results = (
         shape((OUT_PART, ROWS_DEV), BF16),

time: 56.7 us -> 57.3 us (1.011)
  no operation moved by 1% of the time
where the time goes in v5:
time: 57.3 us; the launch traced here: 57.1 us
  Pallas kernels  56.4 us (98%)
  between operations  0.64 us (1%)
    pallas_call x1, Pallas kernels, body(): pl.pallas_call(kernel, out_shape=results, in_specs=[pl.BlockSpec(memory_s...  54.8 us
    pallas_call x1, Pallas kernels, body(): pl.pallas_call(writer, out_shape=results, in_specs=[pl.BlockSpec(memory_s...  1.61 us

profile of v5, /device:TPU:1, one launch (start us, length us, event | category | flops | bytes accessed | tf_op | source)
XLA Modules:
  0.0 57.1 jit_solution(6701438014288763831)
XLA Ops:
  0.6 54.8 %shard_map.119 = (bf16[16,256]{1,0:T(8,128)(2,1)}, f32[32,512]{1,0:T(8,128)}, f32[128,128]{1,0:T(8,128)}, f32[128,128]{1,0:T(8,128)}, f32[64,128]{1,0:T(8,128)}) custom-call(bf16[32,512]{1,0:T(8,128)(2,1)} %sky_in.1, s32[8,512]{1,0:T(8,128)} %nb_in.1, s32[2,128]{1,0:T(2,128)} %sl_in.1, s32[1,128]{1,0:T(1,128)} %bitcast.9, bf16[128,128]{1,0:T(8,128)(2,1)} %bitcast.6, ...), custom_call_target="tpu_custom_call" | custom-call | flops 600000000 | bytes 1000000 | tf_op jit(solution)/shard_map/pallas_call | solution.py:583
  55.5 1.6 %shard_map.120 = (bf16[16,256]{1,0:T(8,128)(2,1)}, f32[32,512]{1,0:T(8,128)}, f32[128,128]{1,0:T(8,128)}, f32[128,128]{1,0:T(8,128)}, f32[64,128]{1,0:T(8,128)}) custom-call(bf16[16,256]{1,0:T(8,128)(2,1)} %get-tuple-element.15.refs_0_, f32[32,512]{1,0:T(8,128)} %get-tuple-element.16.refs_1_, f32[128,128]{1,0:T(8,128)} %get-tuple-element.17.refs_2_, ...), custom_call_target="tpu_custom_call" | custom-call | tf_op jit(solution)/shard_map/pallas_call | solution.py:596

commit v6 on v4

--- a/solution.py
+++ b/solution.py
@@ -427,13 +427,6 @@
     halo_start(5)
 
     local = inner(pair)
-    ig_out[...] = adj0 + finish(5, local)
-
-    rows_t = arrived2(1, B2)
-    result = jnp.zeros((OUT_PART, ROWS_DEV), F32)
-    for s in range(4):
-        result = result + dot(rows_t[s * OUT_PART : (s + 1) * OUT_PART], mmat[s])
-    mo_out[...] = result.astype(BF16)
 
     await_bytes(rg2.at[pl.ds(0, NZ // 2 - 1)], recv.at[G2])
     ft[...] = sum_of(rg2, NZ // 2)
@@ -451,6 +444,13 @@
     @pl.when(jnp.logical_not(holder))
     def _():
         await_bytes(fins, recv.at[I2])
+
+    ig_out[...] = adj0 + finish(5, local)
+    rows_t = arrived2(1, B2)
+    result = jnp.zeros((OUT_PART, ROWS_DEV), F32)
+    for s in range(4):
+        result = result + dot(rows_t[s * OUT_PART : (s + 1) * OUT_PART], mmat[s])
+    mo_out[...] = result.astype(BF16)
 
     scale = 1.0 / math.sqrt(NREGION * ROWS_DEV)
     await_bytes(fin.at[pl.ds(0, NDUO - 1)], recv.at[F2])

time: 56.7 us -> 56.7 us (level)
  no operation moved by 1% of the time
where the time goes in v6:
time: 56.7 us; the launch traced here: 56.5 us
  Pallas kernels  55.9 us (99%)
  between operations  0.64 us (1%)
    pallas_call x1, Pallas kernels, body(): pl.pallas_call(kernel, out_shape=results, in_specs=[pl.BlockSpec(memory_s...  54.3 us
    pallas_call x1, Pallas kernels, body(): pl.pallas_call(writer, out_shape=results, in_specs=[pl.BlockSpec(memory_s...  1.61 us

profile of v6, /device:TPU:1, one launch (start us, length us, event | category | flops | bytes accessed | tf_op | source)
XLA Modules:
  0.0 56.5 jit_solution(4072077412660406076)
XLA Ops:
  0.6 54.3 %shard_map.119 = (bf16[16,256]{1,0:T(8,128)(2,1)}, f32[32,512]{1,0:T(8,128)}, f32[128,128]{1,0:T(8,128)}, f32[128,128]{1,0:T(8,128)}, f32[64,128]{1,0:T(8,128)}) custom-call(bf16[32,512]{1,0:T(8,128)(2,1)} %sky_in.1, s32[8,512]{1,0:T(8,128)} %nb_in.1, s32[2,128]{1,0:T(2,128)} %sl_in.1, s32[1,128]{1,0:T(1,128)} %bitcast.9, bf16[128,128]{1,0:T(8,128)(2,1)} %bitcast.6, ...), custom_call_target="tpu_custom_call" | custom-call | flops 600000000 | bytes 1000000 | tf_op jit(solution)/shard_map/pallas_call | solution.py:556
  54.9 1.6 %shard_map.120 = (bf16[16,256]{1,0:T(8,128)(2,1)}, f32[32,512]{1,0:T(8,128)}, f32[128,128]{1,0:T(8,128)}, f32[128,128]{1,0:T(8,128)}, f32[64,128]{1,0:T(8,128)}) custom-call(bf16[16,256]{1,0:T(8,128)(2,1)} %get-tuple-element.15.refs_0_, f32[32,512]{1,0:T(8,128)} %get-tuple-element.16.refs_1_, f32[128,128]{1,0:T(8,128)} %get-tuple-element.17.refs_2_, ...), custom_call_target="tpu_custom_call" | custom-call | tf_op jit(solution)/shard_map/pallas_call | solution.py:569
